TPU v7x, 512 devices: a whole 4x4x16 slice. The times are simulated.
512 devices in a mesh: dp: 16 (over x, z_hi, core), fsdp: 4 (over y), tensor: 8 (over z_lo).
Axes of the slice: x: 4, y: 4, z: 16 (z_hi: 2, z_lo: 8; z = z_hi * 8 + z_lo), core: 2. Of those that a mesh axis runs over, the one named last changes fastest.
Arguments:
- tokens: bfloat16 [65536, 576], P(('dp', 'fsdp', 'tensor')), may hold values from -6 to 6
- gate_weight: bfloat16 [576, 1536], P('fsdp', 'tensor'), may hold values from -0.25 to 0.25
- up_weight: bfloat16 [576, 1536], P('fsdp', 'tensor'), may hold values from -0.25 to 0.25
- down_weight: bfloat16 [1536, 576], P('tensor', 'fsdp'), may hold values from -0.15625 to 0.15625
- cotangent: bfloat16 [65536, 576], P(('dp', 'fsdp', 'tensor')), may hold values from -0.119628906 to 0.119628906
Outputs:
- mixed: bfloat16 [65536, 576], P(('dp', 'fsdp', 'tensor'))
- grad_tokens: bfloat16 [65536, 576], P(('dp', 'fsdp', 'tensor'))
- grad_gate_weight: bfloat16 [576, 1536], P('fsdp', 'tensor')
- grad_up_weight: bfloat16 [576, 1536], P('fsdp', 'tensor')
- grad_down_weight: bfloat16 [1536, 576], P('tensor', 'fsdp')
All inputs are finite; a program needn't handle non-finite values.
Results may differ from a plain program's by a relative error of at most 0.025.
Values may be sent and summed in bfloat16 or wider, within the bound.
A program may use at most 64 MiB of HBM per device.

v0:
```python
import jax
import jax.numpy as jnp
from jax import lax
from jax.sharding import PartitionSpec as P


def activate(gate_sum, up_sum):
    sig = jax.nn.sigmoid(gate_sum)
    swished = gate_sum * sig
    slopes = up_sum * sig * (1.0 + gate_sum * (1.0 - sig))
    hidden = (swished * up_sum).astype(jnp.bfloat16)
    return (hidden, swished, slopes)


def inner_rows(left, right):
    return lax.dot_general(
        left, right, (((0,), (0,)), ((), ())), preferred_element_type=jnp.float32
    )


def inner_cols(left, right):
    return lax.dot_general(
        left, right, (((1,), (1,)), ((), ())), preferred_element_type=jnp.float32
    )


def reduce_rows(term_fn, own_rows):
    return lax.psum_scatter(
        term_fn(jnp.int32(0), lax.axis_size("tensor") * own_rows).astype(jnp.bfloat16),
        "tensor",
        scatter_dimension=0,
        tiled=True,
    ).astype(jnp.float32)


def per_device(tokens, gate_weight, up_weight, down_weight, cotangent):
    own_rows = tokens.shape[0]
    all_tokens, all_cotangent = (
        lax.all_gather(tokens, "tensor", axis=0, tiled=True),
        lax.all_gather(cotangent, "tensor", axis=0, tiled=True),
    )
    gate_full, up_full = (
        lax.all_gather(gate_weight, "fsdp", axis=0, tiled=True),
        lax.all_gather(up_weight, "fsdp", axis=0, tiled=True),
    )
    down_full = lax.all_gather(down_weight, "fsdp", axis=1, tiled=True)
    gate_sum = jnp.dot(all_tokens, gate_full, preferred_element_type=jnp.float32)
    up_sum = jnp.dot(all_tokens, up_full, preferred_element_type=jnp.float32)
    hidden, swished, slopes = activate(gate_sum, up_sum)

    def output_term(first_row, row_count):
        return jnp.dot(hidden, down_full, preferred_element_type=jnp.float32)

    mixed = reduce_rows(output_term, own_rows).astype(jnp.bfloat16)
    grad_hidden = inner_cols(all_cotangent, down_full)
    grad_gate = (grad_hidden * slopes).astype(jnp.bfloat16)
    grad_up = (grad_hidden * swished).astype(jnp.bfloat16)

    def input_term(first_row, row_count):
        return inner_cols(grad_gate, gate_full) + inner_cols(grad_up, up_full)

    grad_tokens = reduce_rows(input_term, own_rows).astype(jnp.bfloat16)
    stacked = jnp.stack(
        [
            inner_rows(all_tokens, grad_gate),
            inner_rows(all_tokens, grad_up),
            inner_rows(all_cotangent, hidden),
        ],
        axis=0,
    )
    share = lax.psum_scatter(stacked.astype(jnp.bfloat16), "fsdp", scatter_dimension=1, tiled=True)
    summed = lax.psum(share, "dp")
    return (mixed, grad_tokens, summed[0], summed[1], summed[2].T)


def solution(mesh):
    return jax.shard_map(
        per_device,
        mesh=mesh,
        in_specs=(
            P(("dp", "fsdp", "tensor"), None),
            P("fsdp", "tensor"),
            P("fsdp", "tensor"),
            P("tensor", "fsdp"),
            P(("dp", "fsdp", "tensor"), None),
        ),
        out_specs=(
            P(("dp", "fsdp", "tensor"), None),
            P(("dp", "fsdp", "tensor"), None),
            P("fsdp", "tensor"),
            P("fsdp", "tensor"),
            P("tensor", "fsdp"),
        ),
        check_vma=False,
    )
```

profile of v0, /device:TPU:1, one launch (start us, length us, event | category | flops | bytes accessed | tf_op | source)
XLA Modules:
  0.0 558.0 jit_solution(3035401111612240583)
XLA Ops:
  7.2 0.7 all-gather.3.cloned.1.call-update
  7.9 0.7 all-gather.5.cloned.1.call-update
  8.7 11.0 %all_gather.16 = bf16[576,192]{1,0:T(8,128)(2,1)S(1)} all-gather(bf16[144,192]{1,0:T(8,128)(2,1)} %param.6), channel_id=1, replica_groups=mesh['dp'=16,'fsdp'=4,'tensor'=8] {'fsdp'}, dimensions={0}, use_global_device_ids=true | all-gather | bytes 276480 | tf_op jit(solution)/shard_map/all_gather | solution.py:43
  19.7 9.6 %all_gather.17 = bf16[576,192]{1,0:T(8,128)(2,1)S(1)} all-gather(bf16[144,192]{1,0:T(8,128)(2,1)} %param.7), channel_id=1, replica_groups=mesh['dp'=16,'fsdp'=4,'tensor'=8] {'fsdp'}, dimensions={0}, use_global_device_ids=true | all-gather | bytes 276480 | tf_op jit(solution)/shard_map/all_gather | solution.py:44
  29.3 10.2 %all_gather.18 = bf16[192,576]{0,1:T(8,128)(2,1)S(1)} all-gather(bf16[192,144]{0,1:T(8,128)(2,1)} %param.8), channel_id=1, replica_groups=mesh['dp'=16,'fsdp'=4,'tensor'=8] {'fsdp'}, dimensions={1}, use_global_device_ids=true | all-gather | bytes 276480 | tf_op jit(solution)/shard_map/all_gather | solution.py:46
  39.5 32.3 %all-gather.3.cloned.1.call-done = bf16[1024,576]{0,1:T(8,128)(2,1)} async-done(((bf16[128,576]{0,1:T(8,128)(2,1)}), bf16[1024,576]{0,1:T(8,128)(2,1)}) %all-gather.3.cloned.1.call-update) | async-done | bytes 1179664 | tf_op jit(solution)/shard_map/all_gather | solution.py:39
  71.8 2.8 fusion.5
  74.6 1.4 fusion.4
  76.0 55.1 %all-gather.5.cloned.1.call-done = bf16[1024,576]{0,1:T(8,128)(2,1)} async-done(((bf16[128,576]{0,1:T(8,128)(2,1)}), bf16[1024,576]{0,1:T(8,128)(2,1)}) %all-gather.5.cloned.1.call-update) | async-done | bytes 1179664 | tf_op jit(solution)/shard_map/all_gather | solution.py:40
  131.1 2.6 multiply_convert_fusion
  133.7 0.6 fusion.2
  134.3 0.6 fusion.1
  134.9 0.6 fusion
  135.6 1.2 copy.20
  136.8 1.7 reshape.14
  138.6 29.7 %reduce-scatter.14.cloned.1.call-done = bf16[144,576]{1,0:T(8,128)(2,1)} async-done(((bf16[576,576]{1,0:T(8,128)(2,1)}), bf16[144,576]{1,0:T(8,128)(2,1)}) %reduce-scatter.14.cloned.1.call-update) | async-done | bytes 165904
  168.3 1.1 reshape.15
  169.4 0.9 copy.21
  170.4 0.5 convolution_convert_fusion
  170.9 1.5 copy.16
  172.4 0.5 fusion.6
  172.9 0.5 add_convert_fusion
  173.4 1.4 copy.18
  174.8 245.4 %all-reduce.2.cloned.1.call-done = bf16[3,144,192]{1,2,0:T(8,128)(2,1)} async-done(((bf16[3,144,192]{1,2,0:T(8,128)(2,1)}), bf16[3,144,192]{1,2,0:T(8,128)(2,1)}) %all-reduce.2.cloned.1.call-update) | async-done | bytes 165904 | tf_op jit(solution)/shard_map/psum | solution.py:72
  420.3 1.0 slice_bitcast_fusion
  421.3 0.7 copy.15
  422.0 0.7 copy.14
  422.8 0.7 copy.13
  423.5 61.2 %reduce-scatter.10.cloned.1.call-done = bf16[128,576]{1,0:T(8,128)(2,1)} async-done(((bf16[1024,576]{1,0:T(8,128)(2,1)}), bf16[128,576]{1,0:T(8,128)(2,1)}) %reduce-scatter.10.cloned.1.call-update) | async-done | bytes 147472
  484.7 1.7 copy.17
  486.4 63.1 %reduce-scatter.12.cloned.1.call-done = bf16[128,576]{1,0:T(8,128)(2,1)} async-done(((bf16[1024,576]{1,0:T(8,128)(2,1)}), bf16[128,576]{1,0:T(8,128)(2,1)}) %reduce-scatter.12.cloned.1.call-update) | async-done | bytes 147472
  549.5 1.7 copy.19
  (23 shorter events, 0.5 us)
Async XLA Ops:
  7.2 64.6 %all-gather.3.cloned.1.call-start = ((), (), s32[]{:S(2)}) async-start(), calls=%async_computation.3 | async-start | bytes 1327104 | tf_op jit(solution)/shard_map/all_gather | solution.py:39
  7.9 123.2 %all-gather.5.cloned.1.call-start = ((), (), s32[]{:S(2)}) async-start(), calls=%async_computation.4 | async-start | bytes 1327104 | tf_op jit(solution)/shard_map/all_gather | solution.py:40
  8.6 159.7 %reduce-scatter.14.cloned.1.call-start = ((), (), s32[]{:S(2)}) async-start(), calls=%async_computation.8 | async-start | bytes 921600
  39.5 91.5 %copy-start.3 = (bf16[192,576]{0,1:T(8,128)(2,1)}, bf16[192,576]{0,1:T(8,128)(2,1)S(1)}, u32[]{:S(2)}) copy-start(bf16[192,576]{0,1:T(8,128)(2,1)S(1)} %all_gather.18) | copy-start | bytes 663556
  71.8 2.8 copy-start
  131.1 2.6 copy-start.5
  133.6 1.2 copy-start.1
  138.5 31.9 %copy-start.2 = (bf16[1024,192]{0,1:T(8,128)(2,1)S(1)}, bf16[1024,192]{0,1:T(8,128)(2,1)}, u32[]{:S(2)}) copy-start(bf16[1024,192]{0,1:T(8,128)(2,1)} %copy-done.1) | copy-start | bytes 1179652
  138.5 31.9 %copy-start.4 = (bf16[192,576]{0,1:T(8,128)(2,1)S(1)}, bf16[192,576]{0,1:T(8,128)(2,1)}, u32[]{:S(2)}) copy-start(bf16[192,576]{0,1:T(8,128)(2,1)} %copy-done.3) | copy-start | bytes 663556
  138.5 281.7 %all-reduce.2.cloned.1.call-start = ((), (), s32[]{:S(2)}) async-start(), calls=%async_computation.5 | async-start | bytes 589824 | tf_op jit(solution)/shard_map/psum | solution.py:72
  170.4 314.3 %reduce-scatter.10.cloned.1.call-start = ((), (), s32[]{:S(2)}) async-start(), calls=%async_computation.6 | async-start | bytes 1474560
  172.4 377.1 %reduce-scatter.12.cloned.1.call-start = ((), (), s32[]{:S(2)}) async-start(), calls=%async_computation.7 | async-start | bytes 1474560
Sparse Core Ops, SparseCore 0:
  10.0 61.7 all-gather.2
  73.8 57.1 all-gather.4
  138.7 29.6 reduce-scatter.13
  171.1 249.1 all-reduce.1
  423.2 61.4 reduce-scatter.9
  487.6 61.8 reduce-scatter.11
where the time goes:
time: 564 us; the launch traced here: 558 us
  waiting for transfers between devices  488 us (87%)
  blocking collectives  30.8 us (5%)
  local copies, waits for them, and re-layouts  14.4 us (3%)
  between operations  14.2 us (3%)
  matrix products  9.92 us (2%)
    psum x1, waiting for transfers between devices, per_device(): summed = lax.psum(share, 'dp')  245 us
    unnamed x9, waiting for transfers between devices  155 us
    all_gather x1, waiting for transfers between devices, per_device(): lax.all_gather(cotangent, 'tensor', axis=0, tiled=True)  55.1 us
    all_gather x1, waiting for transfers between devices, per_device(): lax.all_gather(tokens, 'tensor', axis=0, tiled=True)  32.3 us
    unnamed x23, local copies, waits for them, and re-layouts  13.4 us
  transfers between devices with their start and end apart: 6, of which 6 were waited for; matrix products, arithmetic and copies ran while one was open for 2% of the time, Pallas kernels for 0%

commit v1 on v0

v1 whole, which is shorter than its diff:
```python
import jax
import jax.numpy as jnp
from jax import lax
from jax.experimental import pallas as pl
from jax.experimental.pallas import tpu as pltpu
from jax.sharding import PartitionSpec as P

MESH = pl.DeviceIdType.MESH
F32 = jnp.float32
BF16 = jnp.bfloat16

D = 576
ROWS = 128
DY = 144
HID = 192
CHUNKS = 3
CROWS = DY // CHUNKS
TILES = 48
PIECE = TILES // 8


def tn(left, right):
    return lax.dot_general(left, right, (((0,), (0,)), ((), ())), preferred_element_type=F32)


def nt(left, right):
    return lax.dot_general(left, right, (((1,), (1,)), ((), ())), preferred_element_type=F32)


def nn(left, right):
    return jnp.dot(left, right, preferred_element_type=F32)


def kernel(
    tok_ref, gate_ref, up_ref, down_ref, cot_ref,
    mixed_ref, gtok_ref, ggate_ref, gup_ref, gdown_ref,
    xs, wpack, wall, ggu, hid, sib_out, own, sib_in, xsend, xrecv,
    ysend, yrecv, zsend, zrecv, tiles, rsrecv, zhsend, zhrecv, fin,
    tok_s, tok_r, fwd_s, fwd_r, wz_s, wz_r, wy_s, wy_r,
    sib_s, sib_r, tr_s, tr_r, gy_s, gy_r, gz_s, gz_r, rs_s, rs_r, zh_s, zh_r, ag_s, ag_r,
):
    dp = lax.axis_index("dp")
    y = lax.axis_index("fsdp")
    zl = lax.axis_index("tensor")
    x, zh, c = dp // 4, (dp // 2) % 2, dp % 2
    z = zh * 8 + zl
    sib_c = 1 - c

    def dev(xx, yy, zz, cc):
        zz = (zz + 16) % 16
        return ((xx % 4) * 4 + (zz // 8) * 2 + cc, yy % 4, zz % 8)

    def group(dx, dc):
        return dev(x + dx, y, z, c if dc == 0 else sib_c)

    block = (zl + x) % 4 + 4 * c
    k_from = jnp.where((block - zl + 8) % 8 == x, 0, 1)
    k_to = (c + zl // 4) % 2
    local = jnp.logical_and(x == 0, k_to == 0)
    remote = jnp.logical_not(local)
    z_from = dev(x, y, z + x - 4 * k_from, (c + k_from) % 2)
    z_to = dev(x, y, z - x + 4 * k_to, zl // 4)
    zh_dev = dev(x, y, z + 8, c)

    def rcopy(src, dst, ssem, rsem, to):
        return pltpu.make_async_remote_copy(
            src_ref=src, dst_ref=dst, send_sem=ssem, recv_sem=rsem, device_id=to, device_id_type=MESH
        )

    barrier = pltpu.get_barrier_semaphore()

    def greet(to):
        pl.semaphore_signal(barrier, inc=1, device_id=to, device_id_type=MESH)

    for dx in range(4):
        for dc in range(2):
            if dx or dc:
                greet(group(dx, dc))
    for d in (1, 2, 3):
        greet(dev(x, y + d, z, c))
    greet(zh_dev)

    @pl.when(remote)
    def _():
        greet(z_from)
        greet(z_to)

    wpack[:, 0:HID] = gate_ref[...]
    wpack[:, HID : 2 * HID] = up_ref[...]
    eye = (
        lax.broadcasted_iota(jnp.int32, (DY, DY), 0) == lax.broadcasted_iota(jnp.int32, (DY, DY), 1)
    ).astype(BF16)
    wpack[:, 2 * HID : 3 * HID] = nt(eye, down_ref[...]).astype(BF16)
    xs[0, 0] = tok_ref[...].T
    xs[1, 0] = cot_ref[...].T

    @pl.when(remote)
    def _():
        pl.semaphore_wait(barrier, 13)

    @pl.when(local)
    def _():
        pl.semaphore_wait(barrier, 11)

    my_rows = pl.multiple_of(y * DY, 16)

    def chunk(ref, base, i):
        return ref.at[pl.ds(pl.multiple_of(base + i * CROWS, 16), CROWS)]

    wz = [
        rcopy(wpack.at[pl.ds(i * CROWS, CROWS)], chunk(wall, my_rows, i), wz_s.at[i], wz_r.at[i], z_to)
        for i in range(CHUNKS)
    ]

    @pl.when(remote)
    def _():
        for cp in wz:
            cp.start()

    tok = {}
    for a in (0, 1):
        for dx in (2, 1, 3):
            tok[a, dx] = rcopy(
                xs.at[a, 0], xs.at[a, 2 * (4 - dx)], tok_s.at[a, dx], tok_r.at[a, 4 - dx], group(dx, 0)
            )
            tok[a, dx].start()
    fwd = {}
    for a in (0, 1):
        fwd[a, 0] = rcopy(xs.at[a, 0], xs.at[a, 1], fwd_s.at[a, 0], fwd_r.at[a, 0], group(0, 1))
        fwd[a, 0].start()

    @pl.when(local)
    def _():
        wall[pl.ds(my_rows, DY), :] = wpack[...]

    wy = {}
    for i in range(CHUNKS):

        @pl.when(remote)
        def _(i=i):
            wz[i].wait_recv()

        for d in (2, 1, 3):
            wy[i, d] = rcopy(
                chunk(wall, my_rows, i), chunk(wall, my_rows, i), wy_s.at[i, d], wy_r.at[i, 4 - d],
                dev(x, y + d, z, c),
            )
            wy[i, d].start()

    def arrived(ref, sem):
        return rcopy(ref, ref, sem, sem, group(0, 1))

    for a in (0, 1):
        for dx in (1, 3, 2):
            arrived(xs.at[a, 2 * dx], tok_r.at[a, dx]).wait_recv()
            fwd[a, dx] = rcopy(
                xs.at[a, 2 * dx], xs.at[a, 2 * dx + 1], fwd_s.at[a, dx], fwd_r.at[a, dx], group(0, 1)
            )
            fwd[a, dx].start()

    for i in range(CHUNKS):
        for d in (1, 3, 2):
            src_rows = pl.multiple_of(((y + d) % 4) * DY, 16)
            arrived(chunk(wall, src_rows, i), wy_r.at[i, d]).wait_recv()

    for dx in (0, 1, 3, 2):
        cols = pl.ds(dx * 256, 256)
        for a in (0, 1):
            fwd[a, dx].wait_recv()
        tokens = jnp.concatenate([xs[0, 2 * dx], xs[0, 2 * dx + 1]], axis=1)
        cots = jnp.concatenate([xs[1, 2 * dx], xs[1, 2 * dx + 1]], axis=1)
        sums = tn(wall[:, 0 : 2 * HID], tokens)
        grad_hidden = tn(wall[:, 2 * HID : 3 * HID], cots)
        gate_sum, up_sum = sums[0:HID], sums[HID : 2 * HID]
        sig = jax.nn.sigmoid(gate_sum)
        swished = gate_sum * sig
        slopes = up_sum * sig * (1.0 + gate_sum * (1.0 - sig))
        hid[:, cols] = (swished * up_sum).astype(BF16)
        ggu[0:HID, cols] = (grad_hidden * slopes).astype(BF16)
        ggu[HID : 2 * HID, cols] = (grad_hidden * swished).astype(BF16)

    gy = {}
    for d in (2, 1, 3, 0):
        rows = pl.ds(pl.multiple_of(((y + d) % 4) * DY, 16), DY)
        tokens = jnp.concatenate([xs[0, s, rows, :] for s in range(8)], axis=1)
        cots = jnp.concatenate([xs[1, s, rows, :] for s in range(8)], axis=1)
        ysend[d, :, 0 : 2 * HID] = nt(tokens, ggu[...]).astype(BF16)
        ysend[d, :, 2 * HID : 3 * HID] = nt(cots, hid[...]).astype(BF16)
        if d:
            gy[d] = rcopy(ysend.at[d], yrecv.at[4 - d], gy_s.at[d], gy_r.at[4 - d], dev(x, y + d, z, c))
            gy[d].start()

    sib = {}
    for dx in (2, 1, 3, 0):
        cols = pl.ds(dx * 256, 256)
        for a in (0, 1):
            part = nn(wall[:, 2 * HID : 3 * HID], hid[:, cols]) if a == 0 else nn(wall[:, 0 : 2 * HID], ggu[:, cols])
            own[a, dx] = part[:, 0:ROWS]
            sib_out[a, dx] = part[:, ROWS : 2 * ROWS].astype(BF16)
            sib[a, dx] = rcopy(
                sib_out.at[a, dx], sib_in.at[a, dx], sib_s.at[a, dx], sib_r.at[a, dx], group(0, 1)
            )
            sib[a, dx].start()
    tr = {}
    for dx in (2, 1, 3):
        for a in (0, 1):
            sib[a, dx].wait_recv()
            xsend[a, dx] = (own[a, dx] + sib_in[a, dx].astype(F32)).astype(BF16)
            tr[a, dx] = rcopy(
                xsend.at[a, dx], xrecv.at[a, 4 - dx], tr_s.at[a, dx], tr_r.at[a, 4 - dx], group(dx, 0)
            )
            tr[a, dx].start()

    for d in (1, 3, 2):
        arrived(yrecv.at[d], gy_r.at[d]).wait_recv()
    zsend[...] = (
        ysend[0].astype(F32) + yrecv[1].astype(F32) + yrecv[2].astype(F32) + yrecv[3].astype(F32)
    ).astype(BF16)
    gz = rcopy(zsend, zrecv, gz_s, gz_r, z_from)

    @pl.when(remote)
    def _():
        gz.start()

    @pl.when(local)
    def _():
        zrecv[...] = zsend[...]

    for a, out in ((0, mixed_ref), (1, gtok_ref)):
        sib[a, 0].wait_recv()
        total = own[a, 0] + sib_in[a, 0].astype(F32)
        for dx in (1, 3, 2):
            arrived(xrecv.at[a, dx], tr_r.at[a, dx]).wait_recv()
            total = total + xrecv[a, dx].astype(F32)
        out[...] = total.T.astype(BF16)

    @pl.when(remote)
    def _():
        gz.wait_recv()

    for r in range(9):
        for q in range(5):
            width = 128 if q < 4 else 64
            tiles[5 * r + q, :, 0:width] = zrecv[16 * r : 16 * r + 16, 128 * q : 128 * q + width]
            if width < 128:
                tiles[5 * r + q, :, width:128] = jnp.zeros((16, 128 - width), BF16)
    for t in range(45, TILES):
        tiles[t] = jnp.zeros((16, 128), BF16)
    me = x * 2 + c
    rs = {}
    for dx in (2, 1, 3, 0):
        for dc in (1, 0):
            if dx or dc:
                rank = ((x + dx) % 4) * 2 + (c if dc == 0 else sib_c)
                slot = ((4 - dx) % 4) * 2 + dc
                rs[dx, dc] = rcopy(
                    tiles.at[pl.ds(rank * PIECE, PIECE)], rsrecv.at[slot], rs_s.at[dx * 2 + dc], rs_r.at[slot],
                    group(dx, dc),
                )
                rs[dx, dc].start()
    total = tiles[pl.ds(me * PIECE, PIECE)].astype(F32)
    for slot in range(1, 8):
        arrived(rsrecv.at[slot], rs_r.at[slot]).wait_recv()
        total = total + rsrecv[slot].astype(F32)
    zhsend[...] = total.astype(BF16)
    zhc = rcopy(zhsend, zhrecv, zh_s, zh_r, zh_dev)
    zhc.start()
    zhc.wait()
    mine = pl.ds(me * PIECE, PIECE)
    fin[mine] = (zhsend[...].astype(F32) + zhrecv[...].astype(F32)).astype(BF16)
    ag = {}
    for dx in (2, 1, 3, 0):
        for dc in (1, 0):
            if dx or dc:
                slot = ((4 - dx) % 4) * 2 + dc
                ag[dx, dc] = rcopy(
                    fin.at[mine], fin.at[mine], ag_s.at[dx * 2 + dc], ag_r.at[slot], group(dx, dc)
                )
                ag[dx, dc].start()
    for dx in range(4):
        for dc in range(2):
            if dx or dc:
                rank = ((x + dx) % 4) * 2 + (c if dc == 0 else sib_c)
                arrived(fin.at[pl.ds(rank * PIECE, PIECE)], ag_r.at[dx * 2 + dc]).wait_recv()

    whole = jnp.concatenate(
        [jnp.concatenate([fin[5 * r + q] for q in range(5)], axis=1) for r in range(9)], axis=0
    )
    ggate_ref[...] = whole[:, 0:HID]
    gup_ref[...] = whole[:, HID : 2 * HID]
    gdown_ref[...] = tn(whole[:, 2 * HID : 3 * HID], eye).astype(BF16)

    @pl.when(remote)
    def _():
        for cp in wz:
            cp.wait_send()
        gz.wait_send()

    for cps in (tok, fwd, wy, gy, sib, tr, rs, ag):
        for cp in cps.values():
            cp.wait_send()


def per_device(tokens, gate_weight, up_weight, down_weight, cotangent):
    dma = pltpu.SemaphoreType.DMA
    vm = pltpu.VMEM
    outs = (
        jax.ShapeDtypeStruct((ROWS, D), BF16),
        jax.ShapeDtypeStruct((ROWS, D), BF16),
        jax.ShapeDtypeStruct((DY, HID), BF16),
        jax.ShapeDtypeStruct((DY, HID), BF16),
        jax.ShapeDtypeStruct((HID, DY), BF16),
    )
    spec = pl.BlockSpec(memory_space=vm)
    return pl.pallas_call(
        kernel,
        out_shape=outs,
        in_specs=[spec] * 5,
        out_specs=[spec] * 5,
        scratch_shapes=[
            vm((2, 8, D, ROWS), BF16),
            vm((DY, 3 * HID), BF16),
            vm((D, 3 * HID), BF16),
            vm((2 * HID, 8 * ROWS), BF16),
            vm((HID, 8 * ROWS), BF16),
            vm((2, 4, D, ROWS), BF16),
            vm((2, 4, D, ROWS), F32),
            vm((2, 4, D, ROWS), BF16),
            vm((2, 4, D, ROWS), BF16),
            vm((2, 4, D, ROWS), BF16),
            vm((4, DY, 3 * HID), BF16),
            vm((4, DY, 3 * HID), BF16),
            vm((DY, 3 * HID), BF16),
            vm((DY, 3 * HID), BF16),
            vm((TILES, 16, 128), BF16),
            vm((8, PIECE, 16, 128), BF16),
            vm((PIECE, 16, 128), BF16),
            vm((PIECE, 16, 128), BF16),
            vm((TILES, 16, 128), BF16),
            dma((2, 4)), dma((2, 4)),
            dma((2, 4)), dma((2, 4)),
            dma((CHUNKS,)), dma((CHUNKS,)),
            dma((CHUNKS, 4)), dma((CHUNKS, 4)),
            dma((2, 4)), dma((2, 4)),
            dma((2, 4)), dma((2, 4)),
            dma((4,)), dma((4,)),
            dma, dma,
            dma((8,)), dma((8,)),
            dma, dma,
            dma((8,)), dma((8,)),
        ],
        compiler_params=pltpu.CompilerParams(
            collective_id=0, has_side_effects=True, vmem_limit_bytes=48 << 20
        ),
        name="swiglu",
    )(tokens, gate_weight, up_weight, down_weight, cotangent)


def solution(mesh):
    return jax.shard_map(
        per_device,
        mesh=mesh,
        in_specs=(
            P(("dp", "fsdp", "tensor"), None),
            P("fsdp", "tensor"),
            P("fsdp", "tensor"),
            P("tensor", "fsdp"),
            P(("dp", "fsdp", "tensor"), None),
        ),
        out_specs=(
            P(("dp", "fsdp", "tensor"), None),
            P(("dp", "fsdp", "tensor"), None),
            P("fsdp", "tensor"),
            P("fsdp", "tensor"),
            P("tensor", "fsdp"),
        ),
        check_vma=False,
    )
```

time: 564 us -> 78.3 us (0.14); the launches traced: 558 us -> 78.1 us
  waiting for transfers between devices: 488 us -> 0 us
  Pallas kernels: 0 us -> 71 us
  blocking collectives: 30.8 us -> 0 us
  between operations: 14.2 us -> 0.68 us
  matrix products: 9.92 us -> 0 us
  local copies, waits for them, and re-layouts: 14.4 us -> 6.42 us
    psum x1 -> x0, waiting for transfers between devices: 245 us -> none  [per_device(): summed = lax.psum(share, 'dp')]
    unnamed x9 -> x0, waiting for transfers between devices: 155 us -> none
    all_gather x2 -> x0, waiting for transfers between devices: 87.3 us -> none  [the longest x1 55.1 us: per_device(): lax.all_gather(cotangent, 'tensor', axis=0, tiled=True)]
    pallas_call x0 -> x1, Pallas kernels: none -> 71 us  [per_device(): pl.pallas_call(kernel, out_shape=outs, in_specs=[spec] * 5, out_specs=[sp...]
    all_gather x3 -> x0, blocking collectives: 30.8 us -> none  [the longest x1 11 us: per_device(): lax.all_gather(gate_weight, 'fsdp', axis=0, tiled=True)]
    dot_general x9 -> x0, matrix products: 9.92 us -> none  [the longest x3 3.5 us: inner_cols(): lax.dot_general(left, right, (((1,), (1,)), ((), ())), preferred_element_...]
    unnamed x23 -> x13, local copies, waits for them, and re-layouts: 13.4 us -> 4.11 us
  transfers between devices with their start and end apart: 6 -> 0, of which waited for: 6 -> 0; matrix products, arithmetic and copies ran while one was open for 2% -> 0% of each run, Pallas kernels for 0% -> 0%
where the time goes in v1:
time: 78.3 us; the launch traced here: 78.1 us
  Pallas kernels  71 us (91%)
  local copies, waits for them, and re-layouts  6.42 us (8%)
    pallas_call x1, Pallas kernels, per_device(): pl.pallas_call(kernel, out_shape=outs, in_specs=[spec] * 5, out_specs=[sp...  71 us
    unnamed x13, local copies, waits for them, and re-layouts  4.11 us
    pallas_call x3, local copies, waits for them, and re-layouts, per_device(): pl.pallas_call(kernel, out_shape=outs, in_specs=[spec] * 5, out_specs=[sp...  2.31 us

profile of v1, /device:TPU:1, one launch (start us, length us, event | category | flops | bytes accessed | tf_op | source)
XLA Modules:
  0.0 78.1 jit_solution(34481162251915138)
XLA Ops:
  0.6 0.0 copy-start.2
  0.6 1.0 %copy.11.down_ref = bf16[192,144]{1,0:T(8,128)(2,1)S(1)} copy(bf16[192,144]{0,1:T(8,128)(2,1)} %param.8) | data formatting | bytes 110592 | tf_op args[3]
  1.7 0.0 copy-done.2
  1.7 0.0 copy-start.3
  1.7 0.2 copy.10.tok_ref
  1.9 0.7 copy-done.3
  2.6 0.0 copy-start
  2.6 0.0 copy-start.1
  2.6 0.2 copy.12.cot_ref
  2.8 0.7 copy-done
  3.5 0.0 copy-done.1
  3.5 71.0 %swiglu.1 = (bf16[128,576]{1,0:T(8,128)(2,1)S(1)}, bf16[128,576]{1,0:T(8,128)(2,1)S(1)}, bf16[144,192]{1,0:T(8,128)(2,1)S(1)}, bf16[144,192]{1,0:T(8,128)(2,1)S(1)}, bf16[192,144]{1,0:T(8,128)(2,1)S(1)}) custom-call(bf16[128,576]{1,0:T(8,128)(2,1)S(1)} %copy.10.tok_ref, bf16[144,192]{1,0:T(8,128)(2,1)S(1)} %copy-done, bf16[144,192]{1,0:T(8,128)(2,1)S(1)} %copy-done.1, ...), custom_call_target="tpu_custom_call" | custom-call | tf_op jit(solution)/shard_map/swiglu/pallas_call | solution.py:315
  74.5 0.8 %copy.13 = bf16[128,576]{0,1:T(8,128)(2,1)} copy(bf16[128,576]{1,0:T(8,128)(2,1)S(1)} %get-tuple-element.5) | data formatting | bytes 294912 | tf_op jit(solution)/shard_map/swiglu/pallas_call | solution.py:315
  75.3 0.7 copy.15
  76.1 0.8 %copy.14 = bf16[128,576]{0,1:T(8,128)(2,1)} copy(bf16[128,576]{1,0:T(8,128)(2,1)S(1)} %get-tuple-element.6) | data formatting | bytes 294912 | tf_op jit(solution)/shard_map/swiglu/pallas_call | solution.py:315
  76.9 0.6 copy.18
  77.5 0.6 copy.19
Async XLA Ops:
  0.6 1.0 %copy-start.2 = (bf16[128,576]{0,1:T(8,128)(2,1)S(1)}, bf16[128,576]{0,1:T(8,128)(2,1)}, u32[]{:S(2)}) copy-start(bf16[128,576]{0,1:T(8,128)(2,1)} %param.5) | copy-start | bytes 442372
  1.7 0.9 %copy-start.3 = (bf16[128,576]{0,1:T(8,128)(2,1)S(1)}, bf16[128,576]{0,1:T(8,128)(2,1)}, u32[]{:S(2)}) copy-start(bf16[128,576]{0,1:T(8,128)(2,1)} %param.9) | copy-start | bytes 442372
  2.6 0.9 %copy-start = (bf16[144,192]{1,0:T(8,128)(2,1)S(1)}, bf16[144,192]{1,0:T(8,128)(2,1)}, u32[]{:S(2)}) copy-start(bf16[144,192]{1,0:T(8,128)(2,1)} %gate_ref.1) | copy-start | bytes 165892
  2.6 0.9 %copy-start.1 = (bf16[144,192]{1,0:T(8,128)(2,1)S(1)}, bf16[144,192]{1,0:T(8,128)(2,1)}, u32[]{:S(2)}) copy-start(bf16[144,192]{1,0:T(8,128)(2,1)} %up_ref.1) | copy-start | bytes 165892

commit v2 on v1

v2 whole, which is shorter than its diff:
```python
import jax
import jax.numpy as jnp
from jax import lax
from jax.experimental import pallas as pl
from jax.experimental.pallas import tpu as pltpu
from jax.sharding import PartitionSpec as P

MESH = pl.DeviceIdType.MESH
F32 = jnp.float32
BF16 = jnp.bfloat16

D = 576
ROWS = 128
DY = 144
HID = 192
TILES = 41
CUTS = (0, 14, 27, 41)
WIDE = 11
HALF = 6


def tn(left, right):
    return lax.dot_general(left, right, (((0,), (0,)), ((), ())), preferred_element_type=F32)


def nt(left, right):
    return lax.dot_general(left, right, (((1,), (1,)), ((), ())), preferred_element_type=F32)


def nn(left, right):
    return jnp.dot(left, right, preferred_element_type=F32)


def store_gate_up(ref, value):
    for r in range(9):
        for q in range(3):
            ref[3 * r + q] = value[16 * r : 16 * r + 16, 128 * q : 128 * q + 128]


def store_down(ref, value):
    for r in range(9):
        ref[27 + r] = value[16 * r : 16 * r + 16, 0:128]
    for i in range(4):
        ref[36 + i] = jnp.concatenate(
            [value[32 * i : 32 * i + 16, 128:192], value[32 * i + 16 : 32 * i + 32, 128:192]], axis=1
        )
    ref[40] = jnp.concatenate([value[128:144, 128:192], jnp.zeros((16, 64), value.dtype)], axis=1)


def load_gate_up(tile):
    return jnp.concatenate(
        [jnp.concatenate([tile(3 * r + q) for q in range(3)], axis=1) for r in range(9)], axis=0
    )


def load_down(tile):
    rows = []
    for r in range(9):
        last = tile(36 + r // 2)
        rows.append(jnp.concatenate([tile(27 + r), last[:, 0:64] if r % 2 == 0 else last[:, 64:128]], axis=1))
    return jnp.concatenate(rows, axis=0)


def kernel(
    tok_ref, gate_ref, up_ref, down_ref, cot_ref,
    mixed_ref, gtok_ref, ggate_ref, gup_ref, gdown_ref,
    xs, win, wmine, wrows, wall, swi, slo, ggu, hid, sib_out, own, sib_in, xsend, xrecv,
    ysend, xyr, zs, zr, zhsend, zhrecv, fin,
    in_s, tok_s, tok_r, fwd_s, fwd_r, wz_s, wz_r, wy_s, wy_r,
    sib_s, sib_r, tr_s, tr_r, xy_s, xy_r, gz_s, gz_r, zh_s, zh_r, ag_s, ag_r,
):
    dp = lax.axis_index("dp")
    y = lax.axis_index("fsdp")
    zl = lax.axis_index("tensor")
    x, zh, c = dp // 4, (dp // 2) % 2, dp % 2
    z = zh * 8 + zl
    sib_c = 1 - c
    home = zl // 4

    def dev(xx, yy, zz, cc):
        zz = (zz + 16) % 16
        return (((xx + 4) % 4) * 4 + (zz // 8) * 2 + cc, (yy + 4) % 4, zz % 8)

    def group(dx, dc):
        return dev(x + dx, y, z, c if dc == 0 else sib_c)

    block = (zl + x) % 4 + 4 * c
    k_from = jnp.where((block - zl + 8) % 8 == x, 0, 1)
    k_to = (c + home) % 2
    local = jnp.logical_and(x == 0, k_to == 0)
    remote = jnp.logical_not(local)
    z_to = dev(x, y, z - x + 4 * k_to, home)
    zh_dev = dev(x, y, z + 8, c)

    shift = [jnp.where(((zl + r) % 4 + 4 * c - zl + 8) % 8 == r, r, r - 4) for r in range(4)]

    def rcopy(src, dst, ssem, rsem, to):
        return pltpu.make_async_remote_copy(
            src_ref=src, dst_ref=dst, send_sem=ssem, recv_sem=rsem, device_id=to, device_id_type=MESH
        )

    inputs = [
        pltpu.make_async_copy(tok_ref, xs.at[0, 0], in_s.at[0]),
        pltpu.make_async_copy(cot_ref, xs.at[1, 0], in_s.at[1]),
        pltpu.make_async_copy(gate_ref, win.at[0], in_s.at[2]),
        pltpu.make_async_copy(up_ref, win.at[1], in_s.at[3]),
        pltpu.make_async_copy(down_ref, win.at[2], in_s.at[4]),
    ]
    for cp in inputs:
        cp.start()

    barrier = pltpu.get_barrier_semaphore()

    def greet(to):
        pl.semaphore_signal(barrier, inc=1, device_id=to, device_id_type=MESH)

    greet(zh_dev)
    for s in (-4, 3, -3, 2, -2, 1, -1):
        greet(dev(x, y, z - s, home))
    for r in (3, 2, 1):
        for h in range(2):
            greet(dev(x, y, z + shift[r], h))

    @pl.when(c != home)
    def _():
        for h in range(2):
            greet(dev(x, y, z - 4, h))

    for dx in (2, 1, 3, 0):
        for d in (2, 1, 3, 0):
            if dx or d:
                greet(dev(x + dx, y + d, z, c))
        greet(group(dx, 1))

    for cp in inputs:
        cp.wait()
    store_gate_up(wmine, jnp.concatenate([win[0], win[1]], axis=1))
    store_down(wmine, win[2])

    @pl.when(c != home)
    def _():
        pl.semaphore_wait(barrier, 35)

    @pl.when(c == home)
    def _():
        pl.semaphore_wait(barrier, 33)

    def cut(ref, i):
        return ref.at[pl.ds(CUTS[i], CUTS[i + 1] - CUTS[i])]

    wz = [
        rcopy(cut(wmine, i), cut(wrows.at[0], i), wz_s.at[i], wz_r.at[i], z_to) for i in range(len(CUTS) - 1)
    ]

    @pl.when(remote)
    def _():
        for cp in wz:
            cp.start()

    tok = {}
    fwd = {}
    for a in (0, 1):
        for dx in (2, 1, 3):
            tok[a, dx] = rcopy(
                xs.at[a, 0], xs.at[a, 2 * (4 - dx)], tok_s.at[a, dx], tok_r.at[a, 4 - dx], group(dx, 0)
            )
            tok[a, dx].start()
    for a in (0, 1):
        fwd[a, 0] = rcopy(xs.at[a, 0], xs.at[a, 1], fwd_s.at[a, 0], fwd_r.at[a, 0], group(0, 1))
        fwd[a, 0].start()

    @pl.when(local)
    def _():
        wrows[0] = wmine[...]

    wy = {}
    for i in range(len(CUTS) - 1):

        @pl.when(remote)
        def _(i=i):
            wz[i].wait_recv()

        for d in (2, 1, 3):
            wy[i, d] = rcopy(
                cut(wrows.at[0], i), cut(wrows.at[4 - d], i), wy_s.at[i, d], wy_r.at[i, 4 - d],
                dev(x, y + d, z, c),
            )
            wy[i, d].start()

    def arrived(ref, sem):
        return rcopy(ref, ref, sem, sem, group(0, 1))

    def pass_on(a):
        for dx in (1, 3, 2):
            arrived(xs.at[a, 2 * dx], tok_r.at[a, dx]).wait_recv()
            fwd[a, dx] = rcopy(
                xs.at[a, 2 * dx], xs.at[a, 2 * dx + 1], fwd_s.at[a, dx], fwd_r.at[a, dx], group(0, 1)
            )
            fwd[a, dx].start()

    def pair(a, dx):
        return jnp.concatenate([xs[a, 2 * dx], xs[a, 2 * dx + 1]], axis=1)

    pass_on(0)
    for i in range(2):
        for d in (1, 3, 2):
            arrived(cut(wrows.at[d], i), wy_r.at[i, d]).wait_recv()
    for d in range(4):
        rows = pl.ds(pl.multiple_of(((y + d) % 4) * DY, 16), DY)
        wall[rows, 0 : 2 * HID] = load_gate_up(lambda t: wrows[d, t])
    for dx in (0, 1, 3, 2):
        cols = pl.ds(dx * 256, 256)
        fwd[0, dx].wait_recv()
        sums = tn(wall[:, 0 : 2 * HID], pair(0, dx))
        gate_sum, up_sum = sums[0:HID], sums[HID : 2 * HID]
        sig = jax.nn.sigmoid(gate_sum)
        swished = gate_sum * sig
        swi[:, cols] = swished
        slo[:, cols] = up_sum * sig * (1.0 + gate_sum * (1.0 - sig))
        hid[:, cols] = (swished * up_sum).astype(BF16)
    pass_on(1)
    for d in (1, 3, 2):
        arrived(cut(wrows.at[d], 2), wy_r.at[2, d]).wait_recv()
    for d in range(4):
        rows = pl.ds(pl.multiple_of(((y + d) % 4) * DY, 16), DY)
        wall[rows, 2 * HID : 3 * HID] = load_down(lambda t: wrows[d, t])
    for dx in (0, 1, 3, 2):
        cols = pl.ds(dx * 256, 256)
        fwd[1, dx].wait_recv()
        grad_hidden = tn(wall[:, 2 * HID : 3 * HID], pair(1, dx))
        ggu[0:HID, cols] = (grad_hidden * slo[:, cols]).astype(BF16)
        ggu[HID : 2 * HID, cols] = (grad_hidden * swi[:, cols]).astype(BF16)

    xy = {}
    for d in (2, 1, 3, 0):
        rows = pl.ds(pl.multiple_of(((y + d) % 4) * DY, 16), DY)
        tokens = jnp.concatenate([xs[0, s, rows, :] for s in range(8)], axis=1)
        cots = jnp.concatenate([xs[1, s, rows, :] for s in range(8)], axis=1)
        store_gate_up(ysend.at[d], nt(tokens, ggu[...]).astype(BF16))
        store_down(ysend.at[d], nt(cots, hid[...]).astype(BF16))
        for dx in (2, 1, 3, 0):
            piece = ysend.at[d, pl.ds(((x + dx) % 4) * 10, WIDE)]
            if d or dx:
                there = ((4 - dx) % 4, (4 - d) % 4)
                xy[dx, d] = rcopy(
                    piece, xyr.at[there[0], there[1]], xy_s.at[dx, d], xy_r.at[there[0], there[1]],
                    dev(x + dx, y + d, z, c),
                )
                xy[dx, d].start()
            else:
                xyr[0, 0] = piece[...]

    sib = {}
    for dx in (2, 1, 3, 0):
        cols = pl.ds(dx * 256, 256)
        for a in (0, 1):
            part = nn(wall[:, 2 * HID : 3 * HID], hid[:, cols]) if a == 0 else nn(wall[:, 0 : 2 * HID], ggu[:, cols])
            own[a, dx] = part[:, 0:ROWS]
            sib_out[a, dx] = part[:, ROWS : 2 * ROWS].astype(BF16)
            sib[a, dx] = rcopy(
                sib_out.at[a, dx], sib_in.at[a, dx], sib_s.at[a, dx], sib_r.at[a, dx], group(0, 1)
            )
            sib[a, dx].start()
    tr = {}
    for dx in (2, 1, 3):
        for a in (0, 1):
            sib[a, dx].wait_recv()
            xsend[a, dx] = (own[a, dx] + sib_in[a, dx].astype(F32)).astype(BF16)
            tr[a, dx] = rcopy(
                xsend.at[a, dx], xrecv.at[a, 4 - dx], tr_s.at[a, dx], tr_r.at[a, 4 - dx], group(dx, 0)
            )

    for dx in (0, 1, 3, 2):
        for d in (0, 1, 3, 2):
            if dx or d:
                arrived(xyr.at[dx, d], xy_r.at[dx, d]).wait_recv()
    gz = {}
    keep = c == home
    for r in (3, 2, 1, 0):
        there = (r - x + 4) % 4
        total = xyr[there, 0].astype(F32)
        for d in (1, 2, 3):
            total = total + xyr[there, d].astype(F32)
        zs[r] = total.astype(BF16)
        slot = shift[r] + 4
        for h in range(2):
            gz[r, h] = rcopy(
                zs.at[r, pl.ds(5 * h, HALF)], zr.at[slot], gz_s.at[r, h], gz_r.at[slot], dev(x, y, z + shift[r], h)
            )
            if r:
                gz[r, h].start()
            else:
                stays = jnp.logical_and(keep, c == h)

                @pl.when(jnp.logical_not(stays))
                def _(h=h):
                    gz[0, h].start()

                @pl.when(stays)
                def _(h=h):
                    zr[4] = zs[0, pl.ds(5 * h, HALF)]

    for dx in (2, 1, 3):
        for a in (0, 1):
            tr[a, dx].start()

    total = None
    for s in (5, 3, 6, 2, 7, 1, 0):
        arrived(zr.at[s], gz_r.at[s]).wait_recv()

    @pl.when(jnp.logical_not(keep))
    def _():
        arrived(zr.at[4], gz_r.at[4]).wait_recv()

    total = zr[0].astype(F32)
    for s in range(1, 8):
        total = total + zr[s].astype(F32)
    zhsend[...] = total.astype(BF16)
    zhc = rcopy(zhsend, zhrecv, zh_s, zh_r, zh_dev)
    zhc.start()

    for a, out in ((0, mixed_ref), (1, gtok_ref)):
        sib[a, 0].wait_recv()
        total = own[a, 0] + sib_in[a, 0].astype(F32)
        for dx in (1, 3, 2):
            arrived(xrecv.at[a, dx], tr_r.at[a, dx]).wait_recv()
            total = total + xrecv[a, dx].astype(F32)
        out[...] = total.astype(BF16)

    zhc.wait()
    me = x * 2 + c
    fin[me] = (zhsend[...].astype(F32) + zhrecv[...].astype(F32)).astype(BF16)
    ag = {}
    for dx in (2, 1, 3, 0):
        for dc in (1, 0):
            if dx or dc:
                slot = ((4 - dx) % 4) * 2 + dc
                ag[dx, dc] = rcopy(fin.at[me], fin.at[me], ag_s.at[dx * 2 + dc], ag_r.at[slot], group(dx, dc))
                ag[dx, dc].start()
    for dx in range(4):
        for dc in range(2):
            if dx or dc:
                rank = ((x + dx) % 4) * 2 + (c if dc == 0 else sib_c)
                arrived(fin.at[rank], ag_r.at[dx * 2 + dc]).wait_recv()

    def summed(t):
        over = min(t // 10, 3)
        half = min((t - 10 * over) // 5, 1)
        return fin[2 * over + half, t - 10 * over - 5 * half]

    whole = load_gate_up(summed)
    ggate_ref[...] = whole[:, 0:HID]
    gup_ref[...] = whole[:, HID : 2 * HID]
    gdown_ref[...] = load_down(summed)

    @pl.when(remote)
    def _():
        for cp in wz:
            cp.wait_send()

    for key, cp in gz.items():
        if key[0]:
            cp.wait_send()
        else:

            @pl.when(jnp.logical_not(jnp.logical_and(keep, c == key[1])))
            def _(cp=cp):
                cp.wait_send()

    for cps in (tok, fwd, wy, xy, sib, tr, ag):
        for cp in cps.values():
            cp.wait_send()


def place(*refs):
    for i, o in zip(refs[:5], refs[5:]):
        o[...] = i[...]


def per_device(tokens, gate_weight, up_weight, down_weight, cotangent):
    dma = pltpu.SemaphoreType.DMA
    vm = pltpu.VMEM
    outs = (
        jax.ShapeDtypeStruct((D, ROWS), BF16),
        jax.ShapeDtypeStruct((D, ROWS), BF16),
        jax.ShapeDtypeStruct((DY, HID), BF16),
        jax.ShapeDtypeStruct((DY, HID), BF16),
        jax.ShapeDtypeStruct((DY, HID), BF16),
    )
    pieces = len(CUTS) - 1
    results = pl.pallas_call(
        kernel,
        out_shape=outs,
        in_specs=[pl.BlockSpec(memory_space=pl.ANY)] * 5,
        out_specs=[pl.BlockSpec(memory_space=vm)] * 5,
        scratch_shapes=[
            vm((2, 8, D, ROWS), BF16),
            vm((3, DY, HID), BF16),
            vm((TILES, 16, 128), BF16),
            vm((4, TILES, 16, 128), BF16),
            vm((D, 3 * HID), BF16),
            vm((HID, 8 * ROWS), F32),
            vm((HID, 8 * ROWS), F32),
            vm((2 * HID, 8 * ROWS), BF16),
            vm((HID, 8 * ROWS), BF16),
            vm((2, 4, D, ROWS), BF16),
            vm((2, 4, D, ROWS), F32),
            vm((2, 4, D, ROWS), BF16),
            vm((2, 4, D, ROWS), BF16),
            vm((2, 4, D, ROWS), BF16),
            vm((4, TILES, 16, 128), BF16),
            vm((4, 4, WIDE, 16, 128), BF16),
            vm((4, WIDE, 16, 128), BF16),
            vm((8, HALF, 16, 128), BF16),
            vm((HALF, 16, 128), BF16),
            vm((HALF, 16, 128), BF16),
            vm((8, HALF, 16, 128), BF16),
            dma((5,)),
            dma((2, 4)), dma((2, 4)),
            dma((2, 4)), dma((2, 4)),
            dma((pieces,)), dma((pieces,)),
            dma((pieces, 4)), dma((pieces, 4)),
            dma((2, 4)), dma((2, 4)),
            dma((2, 4)), dma((2, 4)),
            dma((4, 4)), dma((4, 4)),
            dma((4, 2)), dma((8,)),
            dma, dma,
            dma((8,)), dma((8,)),
        ],
        compiler_params=pltpu.CompilerParams(
            collective_id=0, has_side_effects=True, vmem_limit_bytes=60 << 20
        ),
        name="swiglu",
    )(tokens.T, gate_weight, up_weight, down_weight.T, cotangent.T)
    mixed, gtok, ggate, gup, gdown = pl.pallas_call(
        place,
        out_shape=outs,
        in_specs=[pl.BlockSpec(memory_space=vm)] * 5,
        out_specs=[pl.BlockSpec(memory_space=vm)] * 5,
        name="place",
    )(*results)
    return mixed.T, gtok.T, ggate, gup, gdown.T


def solution(mesh):
    return jax.shard_map(
        per_device,
        mesh=mesh,
        in_specs=(
            P(("dp", "fsdp", "tensor"), None),
            P("fsdp", "tensor"),
            P("fsdp", "tensor"),
            P("tensor", "fsdp"),
            P(("dp", "fsdp", "tensor"), None),
        ),
        out_specs=(
            P(("dp", "fsdp", "tensor"), None),
            P(("dp", "fsdp", "tensor"), None),
            P("fsdp", "tensor"),
            P("fsdp", "tensor"),
            P("tensor", "fsdp"),
        ),
        check_vma=False,
    )
```

time: 78.3 us -> 69.7 us (0.89)
  local copies, waits for them, and re-layouts: 6.42 us -> 0 us
  Pallas kernels: 71 us -> 68.9 us
    unnamed x13 -> x0, local copies, waits for them, and re-layouts: 4.11 us -> none
    pallas_call x3 -> x0, local copies, waits for them, and re-layouts: 2.31 us -> none  [per_device(): pl.pallas_call(kernel, out_shape=outs, in_specs=[spec] * 5, out_specs=[sp...]
    pallas_call x1 -> x2, Pallas kernels: 71 us -> 68.9 us  [the longest x1 67 us: per_device(): pl.pallas_call(kernel, out_shape=outs, in_specs=[pl.BlockSpec(memory_spac...]
where the time goes in v2:
time: 69.7 us; the launch traced here: 69.5 us
  Pallas kernels  68.9 us (99%)
    pallas_call x1, Pallas kernels, per_device(): pl.pallas_call(kernel, out_shape=outs, in_specs=[pl.BlockSpec(memory_spac...  67 us
    pallas_call x1, Pallas kernels, per_device(): pl.pallas_call(place, out_shape=outs, in_specs=[pl.BlockSpec(memory_space...  1.89 us

profile of v2, /device:TPU:1, one launch (start us, length us, event | category | flops | bytes accessed | tf_op | source)
XLA Modules:
  0.0 69.5 jit_solution(8184092758248205248)
XLA Ops:
  0.6 67.0 %swiglu.1 = (bf16[576,128]{1,0:T(8,128)(2,1)}, bf16[576,128]{1,0:T(8,128)(2,1)}, bf16[144,192]{1,0:T(8,128)(2,1)}, bf16[144,192]{1,0:T(8,128)(2,1)}, bf16[144,192]{1,0:T(8,128)(2,1)}) custom-call(bf16[576,128]{1,0:T(8,128)(2,1)} %bitcast.6, bf16[144,192]{1,0:T(8,128)(2,1)} %gate_ref.1, bf16[144,192]{1,0:T(8,128)(2,1)} %up_ref.1, bf16[144,192]{1,0:T(8,128)(2,1)} %bitcast.8, ...), custom_call_target="tpu_custom_call" | custom-call | tf_op jit(solution)/shard_map/swiglu/pallas_call | solution.py:391
  67.6 1.9 %place.1 = (bf16[576,128]{1,0:T(8,128)(2,1)}, bf16[576,128]{1,0:T(8,128)(2,1)}, bf16[144,192]{1,0:T(8,128)(2,1)}, bf16[144,192]{1,0:T(8,128)(2,1)}, bf16[144,192]{1,0:T(8,128)(2,1)}) custom-call(bf16[576,128]{1,0:T(8,128)(2,1)} %get-tuple-element.15.refs_0_, bf16[576,128]{1,0:T(8,128)(2,1)} %get-tuple-element.16.refs_1_, ...), custom_call_target="tpu_custom_call" | custom-call | tf_op jit(solution)/shard_map/place/pallas_call | solution.py:435

commit v3 on v2

--- a/solution.py
+++ b/solution.py
@@ -15,8 +15,16 @@
 HID = 192
 TILES = 41
 CUTS = (0, 14, 27, 41)
-WIDE = 11
+GU_WIDE, DN_WIDE = 7, 4
 HALF = 6
+
+
+def gate_up_start(x):
+    return 7 * x - x // 3
+
+
+def down_start(x):
+    return 4 * x - 2 * (x // 3)
 
 
 def tn(left, right):
@@ -64,10 +72,10 @@
 def kernel(
     tok_ref, gate_ref, up_ref, down_ref, cot_ref,
     mixed_ref, gtok_ref, ggate_ref, gup_ref, gdown_ref,
-    xs, win, wmine, wrows, wall, swi, slo, ggu, hid, sib_out, own, sib_in, xsend, xrecv,
+    xs, win, wmine, wrows, wall, swi, slo, ggu, hid, sib_out, own, sib_in, xsend, xrecv, xopp,
     ysend, xyr, zs, zr, zhsend, zhrecv, fin,
-    in_s, tok_s, tok_r, fwd_s, fwd_r, wz_s, wz_r, wy_s, wy_r,
-    sib_s, sib_r, tr_s, tr_r, xy_s, xy_r, gz_s, gz_r, zh_s, zh_r, ag_s, ag_r,
+    in_s, tok_s, tok_r, fwd_s, fwd_r, wz_s, wz_r, wy_s, wy_r, opp_s, opp_r,
+    sib_s, sib_r, tro_s, tro_r, tr_s, tr_r, xy_s, xy_r, gz_s, gz_r, zh_s, zh_r, ag_s, ag_r, far_sem,
 ):
     dp = lax.axis_index("dp")
     y = lax.axis_index("fsdp")
@@ -114,7 +122,8 @@
     def greet(to):
         pl.semaphore_signal(barrier, inc=1, device_id=to, device_id_type=MESH)
 
-    greet(zh_dev)
+    for s in (4, -4):
+        greet(dev(x, y, z + s, c))
     for s in (-4, 3, -3, 2, -2, 1, -1):
         greet(dev(x, y, z - s, home))
     for r in (3, 2, 1):
@@ -139,11 +148,13 @@
 
     @pl.when(c != home)
     def _():
-        pl.semaphore_wait(barrier, 35)
+        pl.semaphore_wait(barrier, 36)
 
     @pl.when(c == home)
     def _():
-        pl.semaphore_wait(barrier, 33)
+        pl.semaphore_wait(barrier, 34)
+
+    pl.semaphore_signal(far_sem, inc=1, device_id=dev(x, y, z - 4, c), device_id_type=MESH)
 
     def cut(ref, i):
         return ref.at[pl.ds(CUTS[i], CUTS[i + 1] - CUTS[i])]
@@ -158,9 +169,11 @@
             cp.start()
 
     tok = {}
+    opp = {}
     fwd = {}
+    halves = {1: pl.ds(0, D // 2), 3: pl.ds(D // 2, D // 2)}
     for a in (0, 1):
-        for dx in (2, 1, 3):
+        for dx in (1, 3):
             tok[a, dx] = rcopy(
                 xs.at[a, 0], xs.at[a, 2 * (4 - dx)], tok_s.at[a, dx], tok_r.at[a, 4 - dx], group(dx, 0)
             )
@@ -173,7 +186,36 @@
     def _():
         wrows[0] = wmine[...]
 
+    def arrived(ref, sem):
+        return rcopy(ref, ref, sem, sem, group(0, 1))
+
+    def pass_on(a):
+        for dx in (1, 3):
+            arrived(xs.at[a, 2 * dx], tok_r.at[a, dx]).wait_recv()
+            opp[a, dx] = rcopy(
+                xs.at[a, 2 * dx, halves[dx]], xs.at[a, 4, halves[dx]], opp_s.at[a, dx], opp_r.at[a, dx],
+                group(4 - dx, 0),
+            )
+            opp[a, dx].start()
+            fwd[a, dx] = rcopy(
+                xs.at[a, 2 * dx], xs.at[a, 2 * dx + 1], fwd_s.at[a, dx], fwd_r.at[a, dx], group(0, 1)
+            )
+            fwd[a, dx].start()
+
+    def pass_on_opposite(a):
+        for dx in (1, 3):
+            arrived(xs.at[a, 4, halves[dx]], opp_r.at[a, dx]).wait_recv()
+            fwd[a, dx + 3] = rcopy(
+                xs.at[a, 4, halves[dx]], xs.at[a, 5, halves[dx]], fwd_s.at[a, dx + 3], fwd_r.at[a, dx + 3], group(0, 1)
+            )
+            fwd[a, dx + 3].start()
+
+    def wait_pair(a, dx):
+        for k in (dx,) if dx != 2 else (4, 6):
+            fwd[a, k].wait_recv()
+
     wy = {}
+
     for i in range(len(CUTS) - 1):
 
         @pl.when(remote)
@@ -186,22 +228,15 @@
                 dev(x, y + d, z, c),
             )
             wy[i, d].start()
-
-    def arrived(ref, sem):
-        return rcopy(ref, ref, sem, sem, group(0, 1))
-
-    def pass_on(a):
-        for dx in (1, 3, 2):
-            arrived(xs.at[a, 2 * dx], tok_r.at[a, dx]).wait_recv()
-            fwd[a, dx] = rcopy(
-                xs.at[a, 2 * dx], xs.at[a, 2 * dx + 1], fwd_s.at[a, dx], fwd_r.at[a, dx], group(0, 1)
-            )
-            fwd[a, dx].start()
+        if i == 0:
+            pass_on(0)
 
     def pair(a, dx):
         return jnp.concatenate([xs[a, 2 * dx], xs[a, 2 * dx + 1]], axis=1)
 
-    pass_on(0)
+    pass_on(1)
+    pass_on_opposite(0)
+    pass_on_opposite(1)
     for i in range(2):
         for d in (1, 3, 2):
             arrived(cut(wrows.at[d], i), wy_r.at[i, d]).wait_recv()
@@ -210,7 +245,7 @@
         wall[rows, 0 : 2 * HID] = load_gate_up(lambda t: wrows[d, t])
     for dx in (0, 1, 3, 2):
         cols = pl.ds(dx * 256, 256)
-        fwd[0, dx].wait_recv()
+        wait_pair(0, dx)
         sums = tn(wall[:, 0 : 2 * HID], pair(0, dx))
         gate_sum, up_sum = sums[0:HID], sums[HID : 2 * HID]
         sig = jax.nn.sigmoid(gate_sum)
@@ -218,7 +253,31 @@
         swi[:, cols] = swished
         slo[:, cols] = up_sum * sig * (1.0 + gate_sum * (1.0 - sig))
         hid[:, cols] = (swished * up_sum).astype(BF16)
-    pass_on(1)
+    xy = {}
+    for dx in (0, 1, 3, 2):
+        wait_pair(1, dx)
+
+    def spread(k, d, first, start, count):
+        for dx in (2, 1, 3, 0):
+            piece = ysend.at[d, pl.ds(first + start((x + dx) % 4), count)]
+            there = ((4 - dx) % 4, (4 - d) % 4)
+            place = pl.ds(0, count) if k == 0 else pl.ds(GU_WIDE, count)
+            if d or dx:
+                xy[dx, d, k] = rcopy(
+                    piece, xyr.at[there[0], there[1], place], xy_s.at[k, dx, d], xy_r.at[k, there[0], there[1]],
+                    dev(x + dx, y + d, z, c),
+                )
+                xy[dx, d, k].start()
+            else:
+                xyr[0, 0, place] = piece[...]
+
+    def rows_of(a, d):
+        rows = pl.ds(pl.multiple_of(((y + d) % 4) * DY, 16), DY)
+        return jnp.concatenate([xs[a, s, rows, :] for s in range(8)], axis=1)
+
+    for d in (2, 1, 3, 0):
+        store_down(ysend.at[d], nt(rows_of(1, d), hid[...]).astype(BF16))
+        spread(1, d, 27, down_start, DN_WIDE)
     for d in (1, 3, 2):
         arrived(cut(wrows.at[d], 2), wy_r.at[2, d]).wait_recv()
     for d in range(4):
@@ -226,29 +285,12 @@
         wall[rows, 2 * HID : 3 * HID] = load_down(lambda t: wrows[d, t])
     for dx in (0, 1, 3, 2):
         cols = pl.ds(dx * 256, 256)
-        fwd[1, dx].wait_recv()
         grad_hidden = tn(wall[:, 2 * HID : 3 * HID], pair(1, dx))
         ggu[0:HID, cols] = (grad_hidden * slo[:, cols]).astype(BF16)
         ggu[HID : 2 * HID, cols] = (grad_hidden * swi[:, cols]).astype(BF16)
-
-    xy = {}
     for d in (2, 1, 3, 0):
-        rows = pl.ds(pl.multiple_of(((y + d) % 4) * DY, 16), DY)
-        tokens = jnp.concatenate([xs[0, s, rows, :] for s in range(8)], axis=1)
-        cots = jnp.concatenate([xs[1, s, rows, :] for s in range(8)], axis=1)
-        store_gate_up(ysend.at[d], nt(tokens, ggu[...]).astype(BF16))
-        store_down(ysend.at[d], nt(cots, hid[...]).astype(BF16))
-        for dx in (2, 1, 3, 0):
-            piece = ysend.at[d, pl.ds(((x + dx) % 4) * 10, WIDE)]
-            if d or dx:
-                there = ((4 - dx) % 4, (4 - d) % 4)
-                xy[dx, d] = rcopy(
-                    piece, xyr.at[there[0], there[1]], xy_s.at[dx, d], xy_r.at[there[0], there[1]],
-                    dev(x + dx, y + d, z, c),
-                )
-                xy[dx, d].start()
-            else:
-                xyr[0, 0] = piece[...]
+        store_gate_up(ysend.at[d], nt(rows_of(0, d), ggu[...]).astype(BF16))
+        spread(0, d, 0, gate_up_start, GU_WIDE)
 
     sib = {}
     for dx in (2, 1, 3, 0):
@@ -262,18 +304,21 @@
             )
             sib[a, dx].start()
     tr = {}
-    for dx in (2, 1, 3):
-        for a in (0, 1):
-            sib[a, dx].wait_recv()
-            xsend[a, dx] = (own[a, dx] + sib_in[a, dx].astype(F32)).astype(BF16)
-            tr[a, dx] = rcopy(
-                xsend.at[a, dx], xrecv.at[a, 4 - dx], tr_s.at[a, dx], tr_r.at[a, 4 - dx], group(dx, 0)
-            )
+    tro = {}
+    for a in (0, 1):
+        sib[a, 2].wait_recv()
+        xsend[a, 2] = (own[a, 2] + sib_in[a, 2].astype(F32)).astype(BF16)
+        for dx in (1, 3):
+            tro[a, dx] = rcopy(
+                xsend.at[a, 2, halves[dx]], xopp.at[a, halves[dx]], tro_s.at[a, dx], tro_r.at[a, dx], group(dx, 0)
+            )
+            tro[a, dx].start()
 
     for dx in (0, 1, 3, 2):
         for d in (0, 1, 3, 2):
-            if dx or d:
-                arrived(xyr.at[dx, d], xy_r.at[dx, d]).wait_recv()
+            for k, place in ((1, pl.ds(GU_WIDE, DN_WIDE)), (0, pl.ds(0, GU_WIDE))):
+                if dx or d:
+                    arrived(xyr.at[dx, d, place], xy_r.at[k, dx, d]).wait_recv()
     gz = {}
     keep = c == home
     for r in (3, 2, 1, 0):
@@ -281,11 +326,15 @@
         total = xyr[there, 0].astype(F32)
         for d in (1, 2, 3):
             total = total + xyr[there, d].astype(F32)
-        zs[r] = total.astype(BF16)
+        total = total.astype(BF16)
+        zs[r, 0, 0:4] = total[0:4]
+        zs[r, 0, 4:6] = total[7:9]
+        zs[r, 1, 0:4] = total[3:7]
+        zs[r, 1, 4:6] = total[9:11]
         slot = shift[r] + 4
         for h in range(2):
             gz[r, h] = rcopy(
-                zs.at[r, pl.ds(5 * h, HALF)], zr.at[slot], gz_s.at[r, h], gz_r.at[slot], dev(x, y, z + shift[r], h)
+                zs.at[r, h], zr.at[slot], gz_s.at[r, h], gz_r.at[slot], dev(x, y, z + shift[r], h)
             )
             if r:
                 gz[r, h].start()
@@ -298,10 +347,22 @@
 
                 @pl.when(stays)
                 def _(h=h):
-                    zr[4] = zs[0, pl.ds(5 * h, HALF)]
-
-    for dx in (2, 1, 3):
-        for a in (0, 1):
+                    zr[4] = zs[0, h]
+
+    for a in (0, 1):
+        for dx in (1, 3):
+            sib[a, dx].wait_recv()
+            arrived(xopp.at[a, halves[dx]], tro_r.at[a, dx]).wait_recv()
+            part = own[a, dx] + sib_in[a, dx].astype(F32)
+            extra = xopp[a, halves[dx]].astype(F32)
+            if dx == 1:
+                part = jnp.concatenate([part[0 : D // 2] + extra, part[D // 2 : D]], axis=0)
+            else:
+                part = jnp.concatenate([part[0 : D // 2], part[D // 2 : D] + extra], axis=0)
+            xsend[a, dx] = part.astype(BF16)
+            tr[a, dx] = rcopy(
+                xsend.at[a, dx], xrecv.at[a, 4 - dx], tr_s.at[a, dx], tr_r.at[a, 4 - dx], group(dx, 0)
+            )
             tr[a, dx].start()
 
     total = None
@@ -317,12 +378,13 @@
         total = total + zr[s].astype(F32)
     zhsend[...] = total.astype(BF16)
     zhc = rcopy(zhsend, zhrecv, zh_s, zh_r, zh_dev)
+    pl.semaphore_wait(far_sem, 1)
     zhc.start()
 
     for a, out in ((0, mixed_ref), (1, gtok_ref)):
         sib[a, 0].wait_recv()
         total = own[a, 0] + sib_in[a, 0].astype(F32)
-        for dx in (1, 3, 2):
+        for dx in (1, 3):
             arrived(xrecv.at[a, dx], tr_r.at[a, dx]).wait_recv()
             total = total + xrecv[a, dx].astype(F32)
         out[...] = total.astype(BF16)
@@ -344,9 +406,13 @@
                 arrived(fin.at[rank], ag_r.at[dx * 2 + dc]).wait_recv()
 
     def summed(t):
-        over = min(t // 10, 3)
-        half = min((t - 10 * over) // 5, 1)
-        return fin[2 * over + half, t - 10 * over - 5 * half]
+        over = min(t // 7, 3) if t < 27 else min((t - 27) // 4, 3)
+        u = t - gate_up_start(over) if t < 27 else t - 27 - down_start(over)
+        if t < 27:
+            half, u = (0, u) if u < 4 else (1, u - 3)
+        else:
+            half, u = u // 2, 4 + u % 2
+        return fin[2 * over + half, u]
 
     whole = load_gate_up(summed)
     ggate_ref[...] = whole[:, 0:HID]
@@ -367,7 +433,7 @@
             def _(cp=cp):
                 cp.wait_send()
 
-    for cps in (tok, fwd, wy, xy, sib, tr, ag):
+    for cps in (tok, opp, fwd, wy, xy, sib, tro, tr, ag):
         for cp in cps.values():
             cp.wait_send()
 
@@ -408,24 +474,28 @@
             vm((2, 4, D, ROWS), BF16),
             vm((2, 4, D, ROWS), BF16),
             vm((2, 4, D, ROWS), BF16),
+            vm((2, D, ROWS), BF16),
             vm((4, TILES, 16, 128), BF16),
-            vm((4, 4, WIDE, 16, 128), BF16),
-            vm((4, WIDE, 16, 128), BF16),
+            vm((4, 4, GU_WIDE + DN_WIDE, 16, 128), BF16),
+            vm((4, 2, HALF, 16, 128), BF16),
             vm((8, HALF, 16, 128), BF16),
             vm((HALF, 16, 128), BF16),
             vm((HALF, 16, 128), BF16),
             vm((8, HALF, 16, 128), BF16),
             dma((5,)),
             dma((2, 4)), dma((2, 4)),
-            dma((2, 4)), dma((2, 4)),
+            dma((2, 7)), dma((2, 7)),
             dma((pieces,)), dma((pieces,)),
             dma((pieces, 4)), dma((pieces, 4)),
             dma((2, 4)), dma((2, 4)),
             dma((2, 4)), dma((2, 4)),
-            dma((4, 4)), dma((4, 4)),
+            dma((2, 4)), dma((2, 4)),
+            dma((2, 4)), dma((2, 4)),
+            dma((2, 4, 4)), dma((2, 4, 4)),
             dma((4, 2)), dma((8,)),
             dma, dma,
             dma((8,)), dma((8,)),
+            pltpu.SemaphoreType.REGULAR,
         ],
         compiler_params=pltpu.CompilerParams(
             collective_id=0, has_side_effects=True, vmem_limit_bytes=60 << 20

time: 69.7 us -> 67.4 us (0.967)
  Pallas kernels: 68.9 us -> 66.6 us
    pallas_call x1, Pallas kernels: 67 us -> 64.7 us  [per_device(): pl.pallas_call(kernel, out_shape=outs, in_specs=[pl.BlockSpec(memory_spac...]
where the time goes in v3:
time: 67.4 us; the launch traced here: 67.2 us
  Pallas kernels  66.6 us (99%)
    pallas_call x1, Pallas kernels, per_device(): pl.pallas_call(kernel, out_shape=outs, in_specs=[pl.BlockSpec(memory_spac...  64.7 us
    pallas_call x1, Pallas kernels, per_device(): pl.pallas_call(place, out_shape=outs, in_specs=[pl.BlockSpec(memory_space...  1.89 us

profile of v3, /device:TPU:1, one launch (start us, length us, event | category | flops | bytes accessed | tf_op | source)
XLA Modules:
  0.0 67.2 jit_solution(4724761221615318692)
XLA Ops:
  0.6 64.7 %swiglu.1 = (bf16[576,128]{1,0:T(8,128)(2,1)}, bf16[576,128]{1,0:T(8,128)(2,1)}, bf16[144,192]{1,0:T(8,128)(2,1)}, bf16[144,192]{1,0:T(8,128)(2,1)}, bf16[144,192]{1,0:T(8,128)(2,1)}) custom-call(bf16[576,128]{1,0:T(8,128)(2,1)} %bitcast.6, bf16[144,192]{1,0:T(8,128)(2,1)} %gate_ref.1, bf16[144,192]{1,0:T(8,128)(2,1)} %up_ref.1, bf16[144,192]{1,0:T(8,128)(2,1)} %bitcast.8, ...), custom_call_target="tpu_custom_call" | custom-call | tf_op jit(solution)/shard_map/swiglu/pallas_call | solution.py:457
  65.3 1.9 %place.1 = (bf16[576,128]{1,0:T(8,128)(2,1)}, bf16[576,128]{1,0:T(8,128)(2,1)}, bf16[144,192]{1,0:T(8,128)(2,1)}, bf16[144,192]{1,0:T(8,128)(2,1)}, bf16[144,192]{1,0:T(8,128)(2,1)}) custom-call(bf16[576,128]{1,0:T(8,128)(2,1)} %get-tuple-element.15.refs_0_, bf16[576,128]{1,0:T(8,128)(2,1)} %get-tuple-element.16.refs_1_, ...), custom_call_target="tpu_custom_call" | custom-call | tf_op jit(solution)/shard_map/place/pallas_call | solution.py:505

commit v4 on v3

--- a/solution.py
+++ b/solution.py
@@ -14,7 +14,8 @@
 DY = 144
 HID = 192
 TILES = 41
-CUTS = (0, 14, 27, 41)
+CUTS = (0, 7, 14, 21, 27, 34, 41)
+GU_CUTS = 4
 GU_WIDE, DN_WIDE = 7, 4
 HALF = 6
 
@@ -92,13 +93,14 @@
     def group(dx, dc):
         return dev(x + dx, y, z, c if dc == 0 else sib_c)
 
-    block = (zl + x) % 4 + 4 * c
-    k_from = jnp.where((block - zl + 8) % 8 == x, 0, 1)
     k_to = (c + home) % 2
     local = jnp.logical_and(x == 0, k_to == 0)
     remote = jnp.logical_not(local)
-    z_to = dev(x, y, z - x + 4 * k_to, home)
     zh_dev = dev(x, y, z + 8, c)
+
+    def z_to(i):
+        return dev(x, y, z + jnp.where(x == 0, 4 - 8 * (i % 2), 4 * k_to - x), home)
+
 
     shift = [jnp.where(((zl + r) % 4 + 4 * c - zl + 8) % 8 == r, r, r - 4) for r in range(4)]
 
@@ -123,18 +125,13 @@
         pl.semaphore_signal(barrier, inc=1, device_id=to, device_id_type=MESH)
 
     for s in (4, -4):
-        greet(dev(x, y, z + s, c))
-    for s in (-4, 3, -3, 2, -2, 1, -1):
+        for h in range(2):
+            greet(dev(x, y, z + s, h))
+    for s in (3, -3, 2, -2, 1, -1):
         greet(dev(x, y, z - s, home))
     for r in (3, 2, 1):
         for h in range(2):
             greet(dev(x, y, z + shift[r], h))
-
-    @pl.when(c != home)
-    def _():
-        for h in range(2):
-            greet(dev(x, y, z - 4, h))
-
     for dx in (2, 1, 3, 0):
         for d in (2, 1, 3, 0):
             if dx or d:
@@ -146,13 +143,7 @@
     store_gate_up(wmine, jnp.concatenate([win[0], win[1]], axis=1))
     store_down(wmine, win[2])
 
-    @pl.when(c != home)
-    def _():
-        pl.semaphore_wait(barrier, 36)
-
-    @pl.when(c == home)
-    def _():
-        pl.semaphore_wait(barrier, 34)
+    pl.semaphore_wait(barrier, 35)
 
     pl.semaphore_signal(far_sem, inc=1, device_id=dev(x, y, z - 4, c), device_id_type=MESH)
 
@@ -160,7 +151,7 @@
         return ref.at[pl.ds(CUTS[i], CUTS[i + 1] - CUTS[i])]
 
     wz = [
-        rcopy(cut(wmine, i), cut(wrows.at[0], i), wz_s.at[i], wz_r.at[i], z_to) for i in range(len(CUTS) - 1)
+        rcopy(cut(wmine, i), cut(wrows.at[0], i), wz_s.at[i], wz_r.at[i], z_to(i)) for i in range(len(CUTS) - 1)
     ]
 
     @pl.when(remote)
@@ -228,22 +219,24 @@
                 dev(x, y + d, z, c),
             )
             wy[i, d].start()
-        if i == 0:
+        if i == 1:
             pass_on(0)
+        if i == 4:
+            pass_on(1)
 
     def pair(a, dx):
         return jnp.concatenate([xs[a, 2 * dx], xs[a, 2 * dx + 1]], axis=1)
 
-    pass_on(1)
     pass_on_opposite(0)
-    pass_on_opposite(1)
-    for i in range(2):
+    for i in range(GU_CUTS):
         for d in (1, 3, 2):
             arrived(cut(wrows.at[d], i), wy_r.at[i, d]).wait_recv()
     for d in range(4):
         rows = pl.ds(pl.multiple_of(((y + d) % 4) * DY, 16), DY)
         wall[rows, 0 : 2 * HID] = load_gate_up(lambda t: wrows[d, t])
     for dx in (0, 1, 3, 2):
+        if dx == 2:
+            pass_on_opposite(1)
         cols = pl.ds(dx * 256, 256)
         wait_pair(0, dx)
         sums = tn(wall[:, 0 : 2 * HID], pair(0, dx))
@@ -278,8 +271,9 @@
     for d in (2, 1, 3, 0):
         store_down(ysend.at[d], nt(rows_of(1, d), hid[...]).astype(BF16))
         spread(1, d, 27, down_start, DN_WIDE)
-    for d in (1, 3, 2):
-        arrived(cut(wrows.at[d], 2), wy_r.at[2, d]).wait_recv()
+    for i in range(GU_CUTS, len(CUTS) - 1):
+        for d in (1, 3, 2):
+            arrived(cut(wrows.at[d], i), wy_r.at[i, d]).wait_recv()
     for d in range(4):
         rows = pl.ds(pl.multiple_of(((y + d) % 4) * DY, 16), DY)
         wall[rows, 2 * HID : 3 * HID] = load_down(lambda t: wrows[d, t])
@@ -321,7 +315,7 @@
                     arrived(xyr.at[dx, d, place], xy_r.at[k, dx, d]).wait_recv()
     gz = {}
     keep = c == home
-    for r in (3, 2, 1, 0):
+    for r in (0, 3, 1, 2):
         there = (r - x + 4) % 4
         total = xyr[there, 0].astype(F32)
         for d in (1, 2, 3):
@@ -333,8 +327,9 @@
         zs[r, 1, 4:6] = total[9:11]
         slot = shift[r] + 4
         for h in range(2):
+            far = jnp.where(shift[r] == -4, 4 - 8 * h, shift[r])
             gz[r, h] = rcopy(
-                zs.at[r, h], zr.at[slot], gz_s.at[r, h], gz_r.at[slot], dev(x, y, z + shift[r], h)
+                zs.at[r, h], zr.at[slot], gz_s.at[r, h], gz_r.at[slot], dev(x, y, z + far, h)
             )
             if r:
                 gz[r, h].start()

time: 67.4 us -> 65.2 us (0.967)
  Pallas kernels: 66.6 us -> 64.4 us
    pallas_call x1, Pallas kernels: 64.7 us -> 62.5 us  [per_device(): pl.pallas_call(kernel, out_shape=outs, in_specs=[pl.BlockSpec(memory_spac...]
where the time goes in v4:
time: 65.2 us; the launch traced here: 65 us
  Pallas kernels  64.4 us (99%)
    pallas_call x1, Pallas kernels, per_device(): pl.pallas_call(kernel, out_shape=outs, in_specs=[pl.BlockSpec(memory_spac...  62.5 us
    pallas_call x1, Pallas kernels, per_device(): pl.pallas_call(place, out_shape=outs, in_specs=[pl.BlockSpec(memory_space...  1.89 us

profile of v4, /device:TPU:1, one launch (start us, length us, event | category | flops | bytes accessed | tf_op | source)
XLA Modules:
  0.0 65.0 jit_solution(16755660906895368266)
XLA Ops:
  0.6 62.5 %swiglu.1 = (bf16[576,128]{1,0:T(8,128)(2,1)}, bf16[576,128]{1,0:T(8,128)(2,1)}, bf16[144,192]{1,0:T(8,128)(2,1)}, bf16[144,192]{1,0:T(8,128)(2,1)}, bf16[144,192]{1,0:T(8,128)(2,1)}) custom-call(bf16[576,128]{1,0:T(8,128)(2,1)} %bitcast.6, bf16[144,192]{1,0:T(8,128)(2,1)} %gate_ref.1, bf16[144,192]{1,0:T(8,128)(2,1)} %up_ref.1, bf16[144,192]{1,0:T(8,128)(2,1)} %bitcast.8, ...), custom_call_target="tpu_custom_call" | custom-call | tf_op jit(solution)/shard_map/swiglu/pallas_call | solution.py:452
  63.1 1.9 %place.1 = (bf16[576,128]{1,0:T(8,128)(2,1)}, bf16[576,128]{1,0:T(8,128)(2,1)}, bf16[144,192]{1,0:T(8,128)(2,1)}, bf16[144,192]{1,0:T(8,128)(2,1)}, bf16[144,192]{1,0:T(8,128)(2,1)}) custom-call(bf16[576,128]{1,0:T(8,128)(2,1)} %get-tuple-element.15.refs_0_, bf16[576,128]{1,0:T(8,128)(2,1)} %get-tuple-element.16.refs_1_, ...), custom_call_target="tpu_custom_call" | custom-call | tf_op jit(solution)/shard_map/place/pallas_call | solution.py:500

commit v5 on v4

--- a/solution.py
+++ b/solution.py
@@ -16,16 +16,19 @@
 TILES = 41
 CUTS = (0, 7, 14, 21, 27, 34, 41)
 GU_CUTS = 4
-GU_WIDE, DN_WIDE = 7, 4
-HALF = 6
-
-
-def gate_up_start(x):
-    return 7 * x - x // 3
-
-
-def down_start(x):
-    return 4 * x - 2 * (x // 3)
+FIRST = (27, 0, 15)
+WIDE = (4, 4, 3)
+PLACE = (0, 4, 8)
+SPLIT = 80
+PARTS = (0, 1, 2)
+
+
+def start_of(part, x):
+    return (4 * x - 2 * (x // 3), 4 * x - x // 3, 3 * x)[part]
+
+
+def core_start(part, core):
+    return (2 * core, 2 * core, core)[part]
 
 
 def tn(left, right):
@@ -40,10 +43,10 @@
     return jnp.dot(left, right, preferred_element_type=F32)
 
 
-def store_gate_up(ref, value):
-    for r in range(9):
+def store_gate_up(ref, value, row=0):
+    for r in range(value.shape[0] // 16):
         for q in range(3):
-            ref[3 * r + q] = value[16 * r : 16 * r + 16, 128 * q : 128 * q + 128]
+            ref[3 * (r + row) + q] = value[16 * r : 16 * r + 16, 128 * q : 128 * q + 128]
 
 
 def store_down(ref, value):
@@ -250,27 +253,27 @@
     for dx in (0, 1, 3, 2):
         wait_pair(1, dx)
 
-    def spread(k, d, first, start, count):
+    def spread(p, d):
         for dx in (2, 1, 3, 0):
-            piece = ysend.at[d, pl.ds(first + start((x + dx) % 4), count)]
+            piece = ysend.at[d, pl.ds(FIRST[p] + start_of(p, (x + dx) % 4), WIDE[p])]
             there = ((4 - dx) % 4, (4 - d) % 4)
-            place = pl.ds(0, count) if k == 0 else pl.ds(GU_WIDE, count)
+            place = pl.ds(PLACE[p], WIDE[p])
             if d or dx:
-                xy[dx, d, k] = rcopy(
-                    piece, xyr.at[there[0], there[1], place], xy_s.at[k, dx, d], xy_r.at[k, there[0], there[1]],
+                xy[p, dx, d] = rcopy(
+                    piece, xyr.at[there[0], there[1], place], xy_s.at[p, dx, d], xy_r.at[p, there[0], there[1]],
                     dev(x + dx, y + d, z, c),
                 )
-                xy[dx, d, k].start()
+                xy[p, dx, d].start()
             else:
                 xyr[0, 0, place] = piece[...]
 
-    def rows_of(a, d):
-        rows = pl.ds(pl.multiple_of(((y + d) % 4) * DY, 16), DY)
+    def rows_of(a, d, row=0, count=DY):
+        rows = pl.ds(pl.multiple_of(((y + d) % 4) * DY + row, 16), count)
         return jnp.concatenate([xs[a, s, rows, :] for s in range(8)], axis=1)
 
     for d in (2, 1, 3, 0):
         store_down(ysend.at[d], nt(rows_of(1, d), hid[...]).astype(BF16))
-        spread(1, d, 27, down_start, DN_WIDE)
+        spread(0, d)
     for i in range(GU_CUTS, len(CUTS) - 1):
         for d in (1, 3, 2):
             arrived(cut(wrows.at[d], i), wy_r.at[i, d]).wait_recv()
@@ -283,8 +286,11 @@
         ggu[0:HID, cols] = (grad_hidden * slo[:, cols]).astype(BF16)
         ggu[HID : 2 * HID, cols] = (grad_hidden * swi[:, cols]).astype(BF16)
     for d in (2, 1, 3, 0):
-        store_gate_up(ysend.at[d], nt(rows_of(0, d), ggu[...]).astype(BF16))
-        spread(0, d, 0, gate_up_start, GU_WIDE)
+        store_gate_up(ysend.at[d], nt(rows_of(0, d, 0, SPLIT), ggu[...]).astype(BF16))
+        spread(1, d)
+    for d in (2, 1, 3, 0):
+        store_gate_up(ysend.at[d], nt(rows_of(0, d, SPLIT, DY - SPLIT), ggu[...]).astype(BF16), SPLIT // 16)
+        spread(2, d)
 
     sib = {}
     for dx in (2, 1, 3, 0):
@@ -308,41 +314,38 @@
             )
             tro[a, dx].start()
 
-    for dx in (0, 1, 3, 2):
-        for d in (0, 1, 3, 2):
-            for k, place in ((1, pl.ds(GU_WIDE, DN_WIDE)), (0, pl.ds(0, GU_WIDE))):
-                if dx or d:
-                    arrived(xyr.at[dx, d, place], xy_r.at[k, dx, d]).wait_recv()
     gz = {}
     keep = c == home
-    for r in (0, 3, 1, 2):
-        there = (r - x + 4) % 4
-        total = xyr[there, 0].astype(F32)
-        for d in (1, 2, 3):
-            total = total + xyr[there, d].astype(F32)
-        total = total.astype(BF16)
-        zs[r, 0, 0:4] = total[0:4]
-        zs[r, 0, 4:6] = total[7:9]
-        zs[r, 1, 0:4] = total[3:7]
-        zs[r, 1, 4:6] = total[9:11]
-        slot = shift[r] + 4
-        for h in range(2):
-            far = jnp.where(shift[r] == -4, 4 - 8 * h, shift[r])
-            gz[r, h] = rcopy(
-                zs.at[r, h], zr.at[slot], gz_s.at[r, h], gz_r.at[slot], dev(x, y, z + far, h)
-            )
-            if r:
-                gz[r, h].start()
-            else:
-                stays = jnp.logical_and(keep, c == h)
-
-                @pl.when(jnp.logical_not(stays))
-                def _(h=h):
-                    gz[0, h].start()
-
-                @pl.when(stays)
-                def _(h=h):
-                    zr[4] = zs[0, h]
+    for p in PARTS:
+        for dx in (0, 1, 3, 2):
+            for d in (0, 1, 3, 2):
+                if dx or d:
+                    arrived(xyr.at[dx, d, pl.ds(PLACE[p], WIDE[p])], xy_r.at[p, dx, d]).wait_recv()
+        for r in (0, 3, 1, 2):
+            there = (r - x + 4) % 4
+            total = xyr[there, 0, PLACE[p] : PLACE[p] + WIDE[p]].astype(F32)
+            for d in (1, 2, 3):
+                total = total + xyr[there, d, PLACE[p] : PLACE[p] + WIDE[p]].astype(F32)
+            total = total.astype(BF16)
+            slot = shift[r] + 4
+            for h in range(2):
+                zs[p, r, h] = total[core_start(p, h) : core_start(p, h) + 2]
+                far = jnp.where(shift[r] == -4, 4 - 8 * h, shift[r])
+                gz[p, r, h] = rcopy(
+                    zs.at[p, r, h], zr.at[p, slot], gz_s.at[p, r, h], gz_r.at[p, slot], dev(x, y, z + far, h)
+                )
+                if r:
+                    gz[p, r, h].start()
+                else:
+                    stays = jnp.logical_and(keep, c == h)
+
+                    @pl.when(jnp.logical_not(stays))
+                    def _(p=p, h=h):
+                        gz[p, 0, h].start()
+
+                    @pl.when(stays)
+                    def _(p=p, h=h):
+                        zr[p, 4] = zs[p, 0, h]
 
     for a in (0, 1):
         for dx in (1, 3):
@@ -360,21 +363,22 @@
             )
             tr[a, dx].start()
 
-    total = None
-    for s in (5, 3, 6, 2, 7, 1, 0):
-        arrived(zr.at[s], gz_r.at[s]).wait_recv()
-
-    @pl.when(jnp.logical_not(keep))
-    def _():
-        arrived(zr.at[4], gz_r.at[4]).wait_recv()
-
-    total = zr[0].astype(F32)
-    for s in range(1, 8):
-        total = total + zr[s].astype(F32)
-    zhsend[...] = total.astype(BF16)
-    zhc = rcopy(zhsend, zhrecv, zh_s, zh_r, zh_dev)
     pl.semaphore_wait(far_sem, 1)
-    zhc.start()
+    zhc = {}
+    for p in PARTS:
+        for s in (5, 3, 6, 2, 7, 1, 0):
+            arrived(zr.at[p, s], gz_r.at[p, s]).wait_recv()
+
+        @pl.when(jnp.logical_not(keep))
+        def _(p=p):
+            arrived(zr.at[p, 4], gz_r.at[p, 4]).wait_recv()
+
+        total = zr[p, 0].astype(F32)
+        for s in range(1, 8):
+            total = total + zr[p, s].astype(F32)
+        zhsend[p] = total.astype(BF16)
+        zhc[p] = rcopy(zhsend.at[p], zhrecv.at[p], zh_s.at[p], zh_r.at[p], zh_dev)
+        zhc[p].start()
 
     for a, out in ((0, mixed_ref), (1, gtok_ref)):
         sib[a, 0].wait_recv()
@@ -384,30 +388,32 @@
             total = total + xrecv[a, dx].astype(F32)
         out[...] = total.astype(BF16)
 
-    zhc.wait()
     me = x * 2 + c
-    fin[me] = (zhsend[...].astype(F32) + zhrecv[...].astype(F32)).astype(BF16)
     ag = {}
-    for dx in (2, 1, 3, 0):
-        for dc in (1, 0):
-            if dx or dc:
-                slot = ((4 - dx) % 4) * 2 + dc
-                ag[dx, dc] = rcopy(fin.at[me], fin.at[me], ag_s.at[dx * 2 + dc], ag_r.at[slot], group(dx, dc))
-                ag[dx, dc].start()
-    for dx in range(4):
-        for dc in range(2):
-            if dx or dc:
-                rank = ((x + dx) % 4) * 2 + (c if dc == 0 else sib_c)
-                arrived(fin.at[rank], ag_r.at[dx * 2 + dc]).wait_recv()
+    for p in PARTS:
+        zhc[p].wait()
+        fin[me, p] = (zhsend[p].astype(F32) + zhrecv[p].astype(F32)).astype(BF16)
+        for dx in (2, 1, 3, 0):
+            for dc in (1, 0):
+                if dx or dc:
+                    slot = ((4 - dx) % 4) * 2 + dc
+                    ag[p, dx, dc] = rcopy(
+                        fin.at[me, p], fin.at[me, p], ag_s.at[p, dx * 2 + dc], ag_r.at[p, slot], group(dx, dc)
+                    )
+                    ag[p, dx, dc].start()
+    for p in PARTS:
+        for dx in range(4):
+            for dc in range(2):
+                if dx or dc:
+                    rank = ((x + dx) % 4) * 2 + (c if dc == 0 else sib_c)
+                    arrived(fin.at[rank, p], ag_r.at[p, dx * 2 + dc]).wait_recv()
 
     def summed(t):
-        over = min(t // 7, 3) if t < 27 else min((t - 27) // 4, 3)
-        u = t - gate_up_start(over) if t < 27 else t - 27 - down_start(over)
-        if t < 27:
-            half, u = (0, u) if u < 4 else (1, u - 3)
-        else:
-            half, u = u // 2, 4 + u % 2
-        return fin[2 * over + half, u]
+        p = 0 if t >= FIRST[0] else 1 if t < FIRST[2] else 2
+        over = [n for n in range(4) if 0 <= t - FIRST[p] - start_of(p, n) < WIDE[p]][0]
+        u = t - FIRST[p] - start_of(p, over)
+        half = 0 if u < 2 else 1
+        return fin[2 * over + half, p, u - core_start(p, half)]
 
     whole = load_gate_up(summed)
     ggate_ref[...] = whole[:, 0:HID]
@@ -420,11 +426,11 @@
             cp.wait_send()
 
     for key, cp in gz.items():
-        if key[0]:
+        if key[1]:
             cp.wait_send()
         else:
 
-            @pl.when(jnp.logical_not(jnp.logical_and(keep, c == key[1])))
+            @pl.when(jnp.logical_not(jnp.logical_and(keep, c == key[2])))
             def _(cp=cp):
                 cp.wait_send()
 
@@ -471,12 +477,12 @@
             vm((2, 4, D, ROWS), BF16),
             vm((2, D, ROWS), BF16),
             vm((4, TILES, 16, 128), BF16),
-            vm((4, 4, GU_WIDE + DN_WIDE, 16, 128), BF16),
-            vm((4, 2, HALF, 16, 128), BF16),
-            vm((8, HALF, 16, 128), BF16),
-            vm((HALF, 16, 128), BF16),
-            vm((HALF, 16, 128), BF16),
-            vm((8, HALF, 16, 128), BF16),
+            vm((4, 4, sum(WIDE), 16, 128), BF16),
+            vm((3, 4, 2, 2, 16, 128), BF16),
+            vm((3, 8, 2, 16, 128), BF16),
+            vm((3, 2, 16, 128), BF16),
+            vm((3, 2, 16, 128), BF16),
+            vm((8, 3, 2, 16, 128), BF16),
             dma((5,)),
             dma((2, 4)), dma((2, 4)),
             dma((2, 7)), dma((2, 7)),
@@ -486,22 +492,23 @@
             dma((2, 4)), dma((2, 4)),
             dma((2, 4)), dma((2, 4)),
             dma((2, 4)), dma((2, 4)),
-            dma((2, 4, 4)), dma((2, 4, 4)),
-            dma((4, 2)), dma((8,)),
-            dma, dma,
-            dma((8,)), dma((8,)),
+            dma((3, 4, 4)), dma((3, 4, 4)),
+            dma((3, 4, 2)), dma((3, 8)),
+            dma((3,)), dma((3,)),
+            dma((3, 8)), dma((3, 8)),
             pltpu.SemaphoreType.REGULAR,
         ],
         compiler_params=pltpu.CompilerParams(
-            collective_id=0, has_side_effects=True, vmem_limit_bytes=60 << 20
+            collective_id=0, has_side_effects=True, vmem_limit_bytes=40 << 20
         ),
         name="swiglu",
-    )(tokens.T, gate_weight, up_weight, down_weight.T, cotangent.T)
+    )(*[pltpu.with_memory_space_constraint(v, pltpu.HBM) for v in (tokens.T, gate_weight, up_weight, down_weight.T, cotangent.T)])
     mixed, gtok, ggate, gup, gdown = pl.pallas_call(
         place,
         out_shape=outs,
         in_specs=[pl.BlockSpec(memory_space=vm)] * 5,
         out_specs=[pl.BlockSpec(memory_space=vm)] * 5,
+        compiler_params=pltpu.CompilerParams(vmem_limit_bytes=8 << 20),
         name="place",
     )(*results)
     return mixed.T, gtok.T, ggate, gup, gdown.T

time: 65.2 us -> 61.1 us (0.937)
  Pallas kernels: 64.4 us -> 60.4 us
    pallas_call x1, Pallas kernels: 62.5 us -> 59.5 us  [per_device(): pl.pallas_call(kernel, out_shape=outs, in_specs=[pl.BlockSpec(memory_spac...]
    pallas_call x1, Pallas kernels: 1.89 us -> 0.82 us  [per_device(): pl.pallas_call(place, out_shape=outs, in_specs=[pl.BlockSpec(memory_space...]
where the time goes in v5:
time: 61.1 us; the launch traced here: 61 us
  Pallas kernels  60.4 us (99%)
  between operations  0.64 us (1%)
    pallas_call x1, Pallas kernels, per_device(): pl.pallas_call(kernel, out_shape=outs, in_specs=[pl.BlockSpec(memory_spac...  59.5 us

profile of v5, /device:TPU:1, one launch (start us, length us, event | category | flops | bytes accessed | tf_op | source)
XLA Modules:
  0.0 61.0 jit_solution(17075544496001423221)
XLA Ops:
  0.6 59.5 %swiglu.1 = (bf16[576,128]{1,0:T(8,128)(2,1)S(1)}, bf16[576,128]{1,0:T(8,128)(2,1)S(1)}, bf16[144,192]{1,0:T(8,128)(2,1)S(1)}, bf16[144,192]{1,0:T(8,128)(2,1)S(1)}, bf16[144,192]{1,0:T(8,128)(2,1)S(1)}) custom-call(bf16[576,128]{1,0:T(8,128)(2,1)} %bitcast.6, bf16[144,192]{1,0:T(8,128)(2,1)} %gate_ref.1, bf16[144,192]{1,0:T(8,128)(2,1)} %up_ref.1, ...), custom_call_target="tpu_custom_call" | custom-call | tf_op jit(solution)/shard_map/swiglu/pallas_call | solution.py:458
  60.2 0.8 %place.1 = (bf16[576,128]{1,0:T(8,128)(2,1)}, bf16[576,128]{1,0:T(8,128)(2,1)}, bf16[144,192]{1,0:T(8,128)(2,1)}, bf16[144,192]{1,0:T(8,128)(2,1)}, bf16[144,192]{1,0:T(8,128)(2,1)}) custom-call(bf16[576,128]{1,0:T(8,128)(2,1)S(1)} %get-tuple-element.15.refs_0_, bf16[576,128]{1,0:T(8,128)(2,1)S(1)} %get-tuple-element.16.refs_1_, ...), custom_call_target="tpu_custom_call" | custom-call | tf_op jit(solution)/shard_map/place/pallas_call | solution.py:506

commit v6 on v5

v6 whole, which is shorter than its diff:
```python
import jax
import jax.numpy as jnp
from jax import lax
from jax.experimental import pallas as pl
from jax.experimental.pallas import tpu as pltpu
from jax.sharding import PartitionSpec as P

MESH = pl.DeviceIdType.MESH
F32 = jnp.float32
BF16 = jnp.bfloat16

D = 576
ROWS = 128
DY = 144
HID = 192
TILES = 41
CUTS = (0, 7, 14, 21, 27, 34, 41)
GU_CUTS = 4
FIRST = (27, 0, 15)
WIDE = (4, 4, 3)
PLACE = (0, 4, 8)
PARTS = (0, 1, 2)


def start_of(part, x):
    return (4 * x - 2 * (x // 3), 4 * x - x // 3, 3 * x)[part]


def core_start(part, core):
    return (2 * core, 2 * core, core)[part]


def tn(left, right):
    return lax.dot_general(left, right, (((0,), (0,)), ((), ())), preferred_element_type=F32)


def nt(left, right):
    return lax.dot_general(left, right, (((1,), (1,)), ((), ())), preferred_element_type=F32)


def nn(left, right):
    return jnp.dot(left, right, preferred_element_type=F32)


def store_gate_up(ref, value):
    for r in range(9):
        for q in range(3):
            ref[3 * r + q] = value[16 * r : 16 * r + 16, 128 * q : 128 * q + 128]


def store_down(ref, value):
    for r in range(9):
        ref[27 + r] = value[16 * r : 16 * r + 16, 0:128]
    for i in range(4):
        ref[36 + i] = jnp.concatenate(
            [value[32 * i : 32 * i + 16, 128:192], value[32 * i + 16 : 32 * i + 32, 128:192]], axis=1
        )
    ref[40] = jnp.concatenate([value[128:144, 128:192], jnp.zeros((16, 64), value.dtype)], axis=1)


def load_gate_up(tile):
    return jnp.concatenate(
        [jnp.concatenate([tile(3 * r + q) for q in range(3)], axis=1) for r in range(9)], axis=0
    )


def load_down(tile):
    rows = []
    for r in range(9):
        last = tile(36 + r // 2)
        rows.append(jnp.concatenate([tile(27 + r), last[:, 0:64] if r % 2 == 0 else last[:, 64:128]], axis=1))
    return jnp.concatenate(rows, axis=0)


def kernel(
    tok_ref, gate_ref, up_ref, down_ref, cot_ref,
    mixed_ref, gtok_ref, ggate_ref, gup_ref, gdown_ref,
    xs, win, wmine, wrows, wall, swi, slo, ggu, hid, sib_out, own, sib_in, xsend, xrecv, xopp,
    ysend, xyr, zs, zr, zhsend, zhrecv, fin,
    in_s, tok_s, tok_r, fwd_s, fwd_r, wz_s, wz_r, wy_s, wy_r, opp_s, opp_r,
    sib_s, sib_r, tro_s, tro_r, tr_s, tr_r, xy_s, xy_r, gz_s, gz_r, zh_s, zh_r, ag_s, ag_r, far_sem,
):
    dp = lax.axis_index("dp")
    y = lax.axis_index("fsdp")
    zl = lax.axis_index("tensor")
    x, zh, c = dp // 4, (dp // 2) % 2, dp % 2
    z = zh * 8 + zl
    sib_c = 1 - c
    home = zl // 4

    def dev(xx, yy, zz, cc):
        zz = (zz + 16) % 16
        return (((xx + 4) % 4) * 4 + (zz // 8) * 2 + cc, (yy + 4) % 4, zz % 8)

    def group(dx, dc):
        return dev(x + dx, y, z, c if dc == 0 else sib_c)

    k_to = (c + home) % 2
    local = jnp.logical_and(x == 0, k_to == 0)
    remote = jnp.logical_not(local)
    zh_dev = dev(x, y, z + 8, c)

    def z_to(i):
        return dev(x, y, z + jnp.where(x == 0, 4 - 8 * (i % 2), 4 * k_to - x), home)


    shift = [jnp.where(((zl + r) % 4 + 4 * c - zl + 8) % 8 == r, r, r - 4) for r in range(4)]

    def rcopy(src, dst, ssem, rsem, to):
        return pltpu.make_async_remote_copy(
            src_ref=src, dst_ref=dst, send_sem=ssem, recv_sem=rsem, device_id=to, device_id_type=MESH
        )

    inputs = [
        pltpu.make_async_copy(gate_ref, win.at[0], in_s.at[0]),
        pltpu.make_async_copy(up_ref, win.at[1], in_s.at[0]),
        pltpu.make_async_copy(down_ref, win.at[2], in_s.at[0]),
        pltpu.make_async_copy(tok_ref, xs.at[0, 0], in_s.at[1]),
        pltpu.make_async_copy(cot_ref, xs.at[1, 0], in_s.at[1]),
    ]
    for cp in inputs:
        cp.start()

    def arrived(ref, sem):
        rcopy(ref, ref, sem, sem, group(0, 1)).wait_recv()

    def sent(ref, sem):
        rcopy(ref, ref, sem, sem, group(0, 1)).wait_send()

    barrier = pltpu.get_barrier_semaphore()

    def greet(to):
        pl.semaphore_signal(barrier, inc=1, device_id=to, device_id_type=MESH)

    for s in (4, -4):
        for h in range(2):
            greet(dev(x, y, z + s, h))
    for s in (3, -3, 2, -2, 1, -1):
        greet(dev(x, y, z - s, home))
    for r in (3, 2, 1):
        for h in range(2):
            greet(dev(x, y, z + shift[r], h))
    for dx in (2, 1, 3, 0):
        for d in (2, 1, 3, 0):
            if dx or d:
                greet(dev(x + dx, y + d, z, c))
        greet(group(dx, 1))

    pltpu.make_async_copy(win, win, in_s.at[0]).wait()
    store_gate_up(wmine, jnp.concatenate([win[0], win[1]], axis=1))
    store_down(wmine, win[2])
    pltpu.make_async_copy(xs.at[0, pl.ds(0, 2)], xs.at[0, pl.ds(0, 2)], in_s.at[1]).wait()

    pl.semaphore_wait(barrier, 35)

    pl.semaphore_signal(far_sem, inc=1, device_id=dev(x, y, z - 4, c), device_id_type=MESH)

    def cut(ref, i):
        return ref.at[pl.ds(CUTS[i], CUTS[i + 1] - CUTS[i])]

    wz = [
        rcopy(cut(wmine, i), cut(wrows.at[0], i), wz_s, wz_r.at[i], z_to(i)) for i in range(len(CUTS) - 1)
    ]

    @pl.when(remote)
    def _():
        for cp in wz:
            cp.start()

    halves = {1: pl.ds(0, D // 2), 3: pl.ds(D // 2, D // 2)}
    for a in (0, 1):
        for dx in (1, 3):
            rcopy(xs.at[a, 0], xs.at[a, 2 * (4 - dx)], tok_s, tok_r.at[a], group(dx, 0)).start()
    for a in (0, 1):
        rcopy(xs.at[a, 0], xs.at[a, 1], fwd_s, fwd_r.at[a, 0], group(0, 1)).start()

    @pl.when(local)
    def _():
        wrows[0] = wmine[...]

    def pass_on(a):
        arrived(xs.at[a, pl.ds(2, 2)], tok_r.at[a])
        for dx in (1, 3):
            rcopy(
                xs.at[a, 2 * dx, halves[dx]], xs.at[a, 4, halves[dx]], opp_s, opp_r.at[a], group(4 - dx, 0)
            ).start()
            rcopy(xs.at[a, 2 * dx], xs.at[a, 2 * dx + 1], fwd_s, fwd_r.at[a, 1], group(0, 1)).start()

    def pass_on_opposite(a):
        arrived(xs.at[a, 4], opp_r.at[a])
        rcopy(xs.at[a, 4], xs.at[a, 5], fwd_s, fwd_r.at[a, 2], group(0, 1)).start()

    def wait_pair(a, dx):
        if dx != 3:
            arrived(xs.at[a, pl.ds(2, 2)] if dx == 1 else xs.at[a, 5], fwd_r.at[a, dx])

    for i in range(len(CUTS) - 1):

        @pl.when(remote)
        def _(i=i):
            arrived(cut(wrows.at[0], i), wz_r.at[i])

        for d in (2, 1, 3):
            rcopy(
                cut(wrows.at[0], i), cut(wrows.at[4 - d], i), wy_s, wy_r.at[i], dev(x, y + d, z, c)
            ).start()
        if i == 1:
            pass_on(0)
        if i == 4:
            pass_on(1)

    def from_y(i):
        arrived(wrows.at[pl.ds(1, 3), pl.ds(CUTS[i], CUTS[i + 1] - CUTS[i])], wy_r.at[i])

    def pair(a, dx):
        return jnp.concatenate([xs[a, 2 * dx], xs[a, 2 * dx + 1]], axis=1)

    pass_on_opposite(0)
    for i in range(GU_CUTS):
        from_y(i)
    for d in range(4):
        rows = pl.ds(pl.multiple_of(((y + d) % 4) * DY, 16), DY)
        wall[rows, 0 : 2 * HID] = load_gate_up(lambda t: wrows[d, t])
    for dx in (0, 1, 3, 2):
        if dx == 2:
            pass_on_opposite(1)
        cols = pl.ds(dx * 256, 256)
        wait_pair(0, dx)
        sums = tn(wall[:, 0 : 2 * HID], pair(0, dx))
        gate_sum, up_sum = sums[0:HID], sums[HID : 2 * HID]
        sig = jax.nn.sigmoid(gate_sum)
        swished = gate_sum * sig
        swi[:, cols] = swished
        slo[:, cols] = up_sum * sig * (1.0 + gate_sum * (1.0 - sig))
        hid[:, cols] = (swished * up_sum).astype(BF16)
    for dx in (0, 1, 3, 2):
        wait_pair(1, dx)

    def spread(p, d):
        for dx in (2, 1, 3, 0):
            piece = ysend.at[(y + d) % 4, pl.ds(FIRST[p] + start_of(p, (x + dx) % 4), WIDE[p])]
            there = ((4 - dx) % 4) * 4 + (4 - d) % 4
            place = pl.ds(PLACE[p], WIDE[p])
            if d or dx:
                rcopy(piece, xyr.at[there, place], xy_s, xy_r.at[p], dev(x + dx, y + d, z, c)).start()
            else:
                xyr[0, place] = piece[...]

    def all_of(a):
        return jnp.concatenate([xs[a, s] for s in range(8)], axis=1)

    down_grad = nt(all_of(1), hid[...]).astype(BF16)
    for n in range(4):
        store_down(ysend.at[n], down_grad[DY * n : DY * n + DY])
    for d in (2, 1, 3, 0):
        spread(0, d)
    for i in range(GU_CUTS, len(CUTS) - 1):
        from_y(i)
    for d in range(4):
        rows = pl.ds(pl.multiple_of(((y + d) % 4) * DY, 16), DY)
        wall[rows, 2 * HID : 3 * HID] = load_down(lambda t: wrows[d, t])
    for dx in (0, 1, 3, 2):
        cols = pl.ds(dx * 256, 256)
        grad_hidden = tn(wall[:, 2 * HID : 3 * HID], pair(1, dx))
        ggu[0:HID, cols] = (grad_hidden * slo[:, cols]).astype(BF16)
        ggu[HID : 2 * HID, cols] = (grad_hidden * swi[:, cols]).astype(BF16)
    gate_up_grad = nt(all_of(0), ggu[...]).astype(BF16)
    for n in range(4):
        store_gate_up(ysend.at[n], gate_up_grad[DY * n : DY * n + DY])
    for p in (1, 2):
        for d in (2, 1, 3, 0):
            spread(p, d)

    for dx in (2, 1, 3, 0):
        cols = pl.ds(dx * 256, 256)
        for a in (0, 1):
            part = nn(wall[:, 2 * HID : 3 * HID], hid[:, cols]) if a == 0 else nn(wall[:, 0 : 2 * HID], ggu[:, cols])
            own[a, dx] = part[:, 0:ROWS]
            sib_out[dx, a] = part[:, ROWS : 2 * ROWS].astype(BF16)
            rcopy(
                sib_out.at[dx, a], sib_in.at[dx, a], sib_s, sib_r.at[0 if dx == 2 else 1], group(0, 1)
            ).start()
    arrived(sib_in.at[2], sib_r.at[0])
    for a in (0, 1):
        xsend[a, 2] = (own[a, 2] + sib_in[2, a].astype(F32)).astype(BF16)
        for dx in (1, 3):
            rcopy(xsend.at[a, 2, halves[dx]], xopp.at[a, halves[dx]], tro_s, tro_r, group(dx, 0)).start()

    keep = c == home
    for p in PARTS:
        arrived(xyr.at[pl.ds(1, 15), pl.ds(PLACE[p], WIDE[p])], xy_r.at[p])
        for r in (0, 3, 1, 2):
            there = ((r - x + 4) % 4) * 4
            total = xyr[there, PLACE[p] : PLACE[p] + WIDE[p]].astype(F32)
            for d in (1, 2, 3):
                total = total + xyr[there + d, PLACE[p] : PLACE[p] + WIDE[p]].astype(F32)
            total = total.astype(BF16)
            slot = (shift[r] + 8) % 8
            for h in range(2):
                zs[p, r, h] = total[core_start(p, h) : core_start(p, h) + 2]
                far = jnp.where(shift[r] == -4, 4 - 8 * h, shift[r])
                step = rcopy(zs.at[p, r, h], zr.at[p, slot], gz_s, gz_r.at[p], dev(x, y, z + far, h))
                if r:
                    step.start()
                else:
                    stays = jnp.logical_and(keep, c == h)

                    @pl.when(jnp.logical_not(stays))
                    def _(step=step):
                        step.start()

                    @pl.when(stays)
                    def _(p=p, h=h):
                        zr[p, 0] = zs[p, 0, h]

    arrived(sib_in.at[pl.ds(0, 3)], sib_r.at[1])
    arrived(xopp, tro_r)
    for a in (0, 1):
        for dx in (1, 3):
            part = own[a, dx] + sib_in[dx, a].astype(F32)
            extra = xopp[a, halves[dx]].astype(F32)
            if dx == 1:
                part = jnp.concatenate([part[0 : D // 2] + extra, part[D // 2 : D]], axis=0)
            else:
                part = jnp.concatenate([part[0 : D // 2], part[D // 2 : D] + extra], axis=0)
            xsend[a, dx] = part.astype(BF16)
            rcopy(xsend.at[a, dx], xrecv.at[a, (4 - dx) // 2], tr_s, tr_r.at[a], group(dx, 0)).start()

    pl.semaphore_wait(far_sem, 1)
    for p in PARTS:

        @pl.when(keep)
        def _(p=p):
            arrived(zr.at[p, pl.ds(1, 7)], gz_r.at[p])

        @pl.when(jnp.logical_not(keep))
        def _(p=p):
            arrived(zr.at[p], gz_r.at[p])

        total = zr[p, 0].astype(F32)
        for s in range(1, 8):
            total = total + zr[p, s].astype(F32)
        zhsend[p] = total.astype(BF16)
        rcopy(zhsend.at[p], zhrecv.at[p], zh_s, zh_r.at[p], zh_dev).start()

    for a, out in ((0, mixed_ref), (1, gtok_ref)):
        arrived(xrecv.at[a], tr_r.at[a])
        total = own[a, 0] + sib_in[0, a].astype(F32)
        for n in range(2):
            total = total + xrecv[a, n].astype(F32)
        out[...] = total.astype(BF16)

    me = x * 2 + c
    for p in PARTS:
        arrived(zhrecv.at[p], zh_r.at[p])
        fin[me, p] = (zhsend[p].astype(F32) + zhrecv[p].astype(F32)).astype(BF16)
        for dx in (2, 1, 3, 0):
            for dc in (1, 0):
                if dx or dc:
                    rcopy(fin.at[me, p], fin.at[me, p], ag_s, ag_r.at[p], group(dx, dc)).start()
    for p in PARTS:
        arrived(fin.at[pl.ds(0, 7), p], ag_r.at[p])

    def summed(t):
        p = 0 if t >= FIRST[0] else 1 if t < FIRST[2] else 2
        over = [n for n in range(4) if 0 <= t - FIRST[p] - start_of(p, n) < WIDE[p]][0]
        u = t - FIRST[p] - start_of(p, over)
        half = 0 if u < 2 else 1
        return fin[2 * over + half, p, u - core_start(p, half)]

    whole = load_gate_up(summed)
    ggate_ref[...] = whole[:, 0:HID]
    gup_ref[...] = whole[:, HID : 2 * HID]
    gdown_ref[...] = load_down(summed)

    @pl.when(remote)
    def _():
        sent(wmine, wz_s)

    @pl.when(keep)
    def _():
        sent(zr.at[pl.ds(0, 3), pl.ds(1, 7)], gz_s)

    @pl.when(jnp.logical_not(keep))
    def _():
        sent(zr, gz_s)

    sent(xs.at[0, pl.ds(0, 4)], tok_s)
    sent(xs.at[0, pl.ds(0, 2)], opp_s)
    sent(xs.at[0], fwd_s)
    sent(wrows.at[pl.ds(1, 3)], wy_s)
    sent(xyr.at[pl.ds(1, 15)], xy_s)
    sent(sib_out, sib_s)
    sent(xopp, tro_s)
    sent(xrecv, tr_s)
    sent(zhsend, zh_s)
    sent(fin.at[pl.ds(0, 7)], ag_s)


def place(*refs):
    for i, o in zip(refs[:5], refs[5:]):
        o[...] = i[...]


def per_device(tokens, gate_weight, up_weight, down_weight, cotangent):
    dma = pltpu.SemaphoreType.DMA
    vm = pltpu.VMEM
    outs = (
        jax.ShapeDtypeStruct((D, ROWS), BF16),
        jax.ShapeDtypeStruct((D, ROWS), BF16),
        jax.ShapeDtypeStruct((DY, HID), BF16),
        jax.ShapeDtypeStruct((DY, HID), BF16),
        jax.ShapeDtypeStruct((DY, HID), BF16),
    )
    pieces = len(CUTS) - 1
    results = pl.pallas_call(
        kernel,
        out_shape=outs,
        in_specs=[pl.BlockSpec(memory_space=pl.ANY)] * 5,
        out_specs=[pl.BlockSpec(memory_space=vm)] * 5,
        scratch_shapes=[
            vm((2, 8, D, ROWS), BF16),
            vm((3, DY, HID), BF16),
            vm((TILES, 16, 128), BF16),
            vm((4, TILES, 16, 128), BF16),
            vm((D, 3 * HID), BF16),
            vm((HID, 8 * ROWS), F32),
            vm((HID, 8 * ROWS), F32),
            vm((2 * HID, 8 * ROWS), BF16),
            vm((HID, 8 * ROWS), BF16),
            vm((4, 2, D, ROWS), BF16),
            vm((2, 4, D, ROWS), F32),
            vm((4, 2, D, ROWS), BF16),
            vm((2, 4, D, ROWS), BF16),
            vm((2, 2, D, ROWS), BF16),
            vm((2, D, ROWS), BF16),
            vm((4, TILES, 16, 128), BF16),
            vm((16, sum(WIDE), 16, 128), BF16),
            vm((3, 4, 2, 2, 16, 128), BF16),
            vm((3, 8, 2, 16, 128), BF16),
            vm((3, 2, 16, 128), BF16),
            vm((3, 2, 16, 128), BF16),
            vm((8, 3, 2, 16, 128), BF16),
            dma((2,)),
            dma, dma((2,)),
            dma, dma((2, 3)),
            dma, dma((pieces,)),
            dma, dma((pieces,)),
            dma, dma((2,)),
            dma, dma((2,)),
            dma, dma,
            dma, dma((2,)),
            dma, dma((3,)),
            dma, dma((3,)),
            dma, dma((3,)),
            dma, dma((3,)),
            pltpu.SemaphoreType.REGULAR,
        ],
        compiler_params=pltpu.CompilerParams(
            collective_id=0, has_side_effects=True, vmem_limit_bytes=40 << 20
        ),
        name="swiglu",
    )(*[pltpu.with_memory_space_constraint(v, pltpu.HBM) for v in (tokens.T, gate_weight, up_weight, down_weight.T, cotangent.T)])
    mixed, gtok, ggate, gup, gdown = pl.pallas_call(
        place,
        out_shape=outs,
        in_specs=[pl.BlockSpec(memory_space=vm)] * 5,
        out_specs=[pl.BlockSpec(memory_space=vm)] * 5,
        compiler_params=pltpu.CompilerParams(vmem_limit_bytes=8 << 20),
        name="place",
    )(*results)
    return mixed.T, gtok.T, ggate, gup, gdown.T


def solution(mesh):
    return jax.shard_map(
        per_device,
        mesh=mesh,
        in_specs=(
            P(("dp", "fsdp", "tensor"), None),
            P("fsdp", "tensor"),
            P("fsdp", "tensor"),
            P("tensor", "fsdp"),
            P(("dp", "fsdp", "tensor"), None),
        ),
        out_specs=(
            P(("dp", "fsdp", "tensor"), None),
            P(("dp", "fsdp", "tensor"), None),
            P("fsdp", "tensor"),
            P("fsdp", "tensor"),
            P("tensor", "fsdp"),
        ),
        check_vma=False,
    )
```

time: 61.1 us -> 58.6 us (0.959)
  Pallas kernels: 60.4 us -> 57.8 us
    pallas_call x1, Pallas kernels: 59.5 us -> 57 us  [per_device(): pl.pallas_call(kernel, out_shape=outs, in_specs=[pl.BlockSpec(memory_spac...]
where the time goes in v6:
time: 58.6 us; the launch traced here: 58.4 us
  Pallas kernels  57.8 us (99%)
  between operations  0.64 us (1%)
    pallas_call x1, Pallas kernels, per_device(): pl.pallas_call(kernel, out_shape=outs, in_specs=[pl.BlockSpec(memory_spac...  57 us

profile of v6, /device:TPU:1, one launch (start us, length us, event | category | flops | bytes accessed | tf_op | source)
XLA Modules:
  0.0 58.4 jit_solution(2210926863516816061)
XLA Ops:
  0.6 57.0 %swiglu.1 = (bf16[576,128]{1,0:T(8,128)(2,1)S(1)}, bf16[576,128]{1,0:T(8,128)(2,1)S(1)}, bf16[144,192]{1,0:T(8,128)(2,1)S(1)}, bf16[144,192]{1,0:T(8,128)(2,1)S(1)}, bf16[144,192]{1,0:T(8,128)(2,1)S(1)}) custom-call(bf16[576,128]{1,0:T(8,128)(2,1)} %bitcast.6, bf16[144,192]{1,0:T(8,128)(2,1)} %gate_ref.1, bf16[144,192]{1,0:T(8,128)(2,1)} %up_ref.1, ...), custom_call_target="tpu_custom_call" | custom-call | tf_op jit(solution)/shard_map/swiglu/pallas_call | solution.py:416
  57.6 0.8 %place.1 = (bf16[576,128]{1,0:T(8,128)(2,1)}, bf16[576,128]{1,0:T(8,128)(2,1)}, bf16[144,192]{1,0:T(8,128)(2,1)}, bf16[144,192]{1,0:T(8,128)(2,1)}, bf16[144,192]{1,0:T(8,128)(2,1)}) custom-call(bf16[576,128]{1,0:T(8,128)(2,1)S(1)} %get-tuple-element.15.refs_0_, bf16[576,128]{1,0:T(8,128)(2,1)S(1)} %get-tuple-element.16.refs_1_, ...), custom_call_target="tpu_custom_call" | custom-call | tf_op jit(solution)/shard_map/place/pallas_call | solution.py:464

commit v7 on v6

--- a/solution.py
+++ b/solution.py
@@ -76,9 +76,9 @@
     tok_ref, gate_ref, up_ref, down_ref, cot_ref,
     mixed_ref, gtok_ref, ggate_ref, gup_ref, gdown_ref,
     xs, win, wmine, wrows, wall, swi, slo, ggu, hid, sib_out, own, sib_in, xsend, xrecv, xopp,
-    ysend, xyr, zs, zr, zhsend, zhrecv, fin,
+    ysend, down_early, xyr, zs, zr, zhsend, zhrecv, fin,
     in_s, tok_s, tok_r, fwd_s, fwd_r, wz_s, wz_r, wy_s, wy_r, opp_s, opp_r,
-    sib_s, sib_r, tro_s, tro_r, tr_s, tr_r, xy_s, xy_r, gz_s, gz_r, zh_s, zh_r, ag_s, ag_r, far_sem,
+    sib_s, sib_r, tro_s, tro_r, tr_s, tr_r, xy_s, xy_r, gz_s, gz_r, zh_s, zh_r, ag_s, ag_r,
 ):
     dp = lax.axis_index("dp")
     y = lax.axis_index("fsdp")
@@ -98,13 +98,12 @@
     k_to = (c + home) % 2
     local = jnp.logical_and(x == 0, k_to == 0)
     remote = jnp.logical_not(local)
-    zh_dev = dev(x, y, z + 8, c)
 
     def z_to(i):
         return dev(x, y, z + jnp.where(x == 0, 4 - 8 * (i % 2), 4 * k_to - x), home)
 
 
-    shift = [jnp.where(((zl + r) % 4 + 4 * c - zl + 8) % 8 == r, r, r - 4) for r in range(4)]
+    shift = [jnp.where(((zl + r) % 4 + 4 * c - zl + 8) % 8 == r, r - 4, r) for r in range(4)]
 
     def rcopy(src, dst, ssem, rsem, to):
         return pltpu.make_async_remote_copy(
@@ -132,28 +131,32 @@
     def greet(to):
         pl.semaphore_signal(barrier, inc=1, device_id=to, device_id_type=MESH)
 
-    for s in (4, -4):
+    for dx in (1, 3):
+        greet(group(dx, 0))
+    for s in (4, -4, 3, -3, 2, -2, 1, -1):
         for h in range(2):
             greet(dev(x, y, z + s, h))
-    for s in (3, -3, 2, -2, 1, -1):
-        greet(dev(x, y, z - s, home))
-    for r in (3, 2, 1):
-        for h in range(2):
-            greet(dev(x, y, z + shift[r], h))
     for dx in (2, 1, 3, 0):
         for d in (2, 1, 3, 0):
-            if dx or d:
+            if d or dx == 2:
                 greet(dev(x + dx, y + d, z, c))
         greet(group(dx, 1))
+
+    pltpu.make_async_copy(xs.at[0, pl.ds(0, 2)], xs.at[0, pl.ds(0, 2)], in_s.at[1]).wait()
+    pl.semaphore_wait(barrier, 35)
+
+    halves = {1: pl.ds(0, D // 2), 3: pl.ds(D // 2, D // 2)}
+    for a in (0, 1):
+        for late in (0, 1):
+            for dx in (1, 3):
+                rows = halves[dx if late else 4 - dx]
+                rcopy(
+                    xs.at[a, 0, rows], xs.at[a, 2 * (4 - dx), rows], tok_s, tok_r.at[a, late], group(dx, 0)
+                ).start()
 
     pltpu.make_async_copy(win, win, in_s.at[0]).wait()
     store_gate_up(wmine, jnp.concatenate([win[0], win[1]], axis=1))
     store_down(wmine, win[2])
-    pltpu.make_async_copy(xs.at[0, pl.ds(0, 2)], xs.at[0, pl.ds(0, 2)], in_s.at[1]).wait()
-
-    pl.semaphore_wait(barrier, 35)
-
-    pl.semaphore_signal(far_sem, inc=1, device_id=dev(x, y, z - 4, c), device_id_type=MESH)
 
     def cut(ref, i):
         return ref.at[pl.ds(CUTS[i], CUTS[i + 1] - CUTS[i])]
@@ -167,10 +170,6 @@
         for cp in wz:
             cp.start()
 
-    halves = {1: pl.ds(0, D // 2), 3: pl.ds(D // 2, D // 2)}
-    for a in (0, 1):
-        for dx in (1, 3):
-            rcopy(xs.at[a, 0], xs.at[a, 2 * (4 - dx)], tok_s, tok_r.at[a], group(dx, 0)).start()
     for a in (0, 1):
         rcopy(xs.at[a, 0], xs.at[a, 1], fwd_s, fwd_r.at[a, 0], group(0, 1)).start()
 
@@ -178,13 +177,13 @@
     def _():
         wrows[0] = wmine[...]
 
-    def pass_on(a):
-        arrived(xs.at[a, pl.ds(2, 2)], tok_r.at[a])
+    def pass_on(a, late):
+        arrived(xs.at[a, 2], tok_r.at[a, late])
         for dx in (1, 3):
-            rcopy(
-                xs.at[a, 2 * dx, halves[dx]], xs.at[a, 4, halves[dx]], opp_s, opp_r.at[a], group(4 - dx, 0)
-            ).start()
-            rcopy(xs.at[a, 2 * dx], xs.at[a, 2 * dx + 1], fwd_s, fwd_r.at[a, 1], group(0, 1)).start()
+            rows = halves[4 - dx if late else dx]
+            if not late:
+                rcopy(xs.at[a, 2 * dx, rows], xs.at[a, 4, rows], opp_s, opp_r.at[a], group(4 - dx, 0)).start()
+            rcopy(xs.at[a, 2 * dx, rows], xs.at[a, 2 * dx + 1, rows], fwd_s, fwd_r.at[a, 1], group(0, 1)).start()
 
     def pass_on_opposite(a):
         arrived(xs.at[a, 4], opp_r.at[a])
@@ -204,10 +203,8 @@
             rcopy(
                 cut(wrows.at[0], i), cut(wrows.at[4 - d], i), wy_s, wy_r.at[i], dev(x, y + d, z, c)
             ).start()
-        if i == 1:
-            pass_on(0)
-        if i == 4:
-            pass_on(1)
+        if i in (0, 2, 4, 5):
+            pass_on(int(i > 2), int(i in (2, 5)))
 
     def from_y(i):
         arrived(wrows.at[pl.ds(1, 3), pl.ds(CUTS[i], CUTS[i + 1] - CUTS[i])], wy_r.at[i])
@@ -233,8 +230,11 @@
         swi[:, cols] = swished
         slo[:, cols] = up_sum * sig * (1.0 + gate_sum * (1.0 - sig))
         hid[:, cols] = (swished * up_sum).astype(BF16)
-    for dx in (0, 1, 3, 2):
+    for dx in (0, 1, 3):
         wait_pair(1, dx)
+    early = jnp.concatenate([xs[1, n] for n in (0, 1, 2, 3, 6, 7)], axis=1)
+    down_early[...] = nt(early, jnp.concatenate([hid[:, 0:512], hid[:, 768:1024]], axis=1))
+    wait_pair(1, 2)
 
     def spread(p, d):
         for dx in (2, 1, 3, 0):
@@ -246,10 +246,7 @@
             else:
                 xyr[0, place] = piece[...]
 
-    def all_of(a):
-        return jnp.concatenate([xs[a, s] for s in range(8)], axis=1)
-
-    down_grad = nt(all_of(1), hid[...]).astype(BF16)
+    down_grad = (down_early[...] + nt(pair(1, 2), hid[:, 512:768])).astype(BF16)
     for n in range(4):
         store_down(ysend.at[n], down_grad[DY * n : DY * n + DY])
     for d in (2, 1, 3, 0):
@@ -264,7 +261,7 @@
         grad_hidden = tn(wall[:, 2 * HID : 3 * HID], pair(1, dx))
         ggu[0:HID, cols] = (grad_hidden * slo[:, cols]).astype(BF16)
         ggu[HID : 2 * HID, cols] = (grad_hidden * swi[:, cols]).astype(BF16)
-    gate_up_grad = nt(all_of(0), ggu[...]).astype(BF16)
+    gate_up_grad = nt(jnp.concatenate([xs[0, n] for n in range(8)], axis=1), ggu[...]).astype(BF16)
     for n in range(4):
         store_gate_up(ysend.at[n], gate_up_grad[DY * n : DY * n + DY])
     for p in (1, 2):
@@ -286,7 +283,7 @@
         for dx in (1, 3):
             rcopy(xsend.at[a, 2, halves[dx]], xopp.at[a, halves[dx]], tro_s, tro_r, group(dx, 0)).start()
 
-    keep = c == home
+    keep = c != home
     for p in PARTS:
         arrived(xyr.at[pl.ds(1, 15), pl.ds(PLACE[p], WIDE[p])], xy_r.at[p])
         for r in (0, 3, 1, 2):
@@ -326,7 +323,6 @@
             xsend[a, dx] = part.astype(BF16)
             rcopy(xsend.at[a, dx], xrecv.at[a, (4 - dx) // 2], tr_s, tr_r.at[a], group(dx, 0)).start()
 
-    pl.semaphore_wait(far_sem, 1)
     for p in PARTS:
 
         @pl.when(keep)
@@ -341,8 +337,17 @@
         for s in range(1, 8):
             total = total + zr[p, s].astype(F32)
         zhsend[p] = total.astype(BF16)
-        rcopy(zhsend.at[p], zhrecv.at[p], zh_s, zh_r.at[p], zh_dev).start()
-
+        for n in range(2):
+            rcopy(zhsend.at[p], zhrecv.at[p, n], zh_s, zh_r.at[p], dev(x, y, z + 4 - 8 * n, c)).start()
+
+    me = x * 2 + c
+    for p in PARTS:
+        arrived(zhrecv.at[p], zh_r.at[p])
+        fin[me, p] = (zhrecv[p, 0].astype(F32) + zhrecv[p, 1].astype(F32)).astype(BF16)
+        for dx in (2, 1, 3, 0):
+            for dc in (1, 0):
+                if dx or dc:
+                    rcopy(fin.at[me, p], fin.at[me, p], ag_s, ag_r.at[p], group(dx, dc)).start()
     for a, out in ((0, mixed_ref), (1, gtok_ref)):
         arrived(xrecv.at[a], tr_r.at[a])
         total = own[a, 0] + sib_in[0, a].astype(F32)
@@ -350,14 +355,6 @@
             total = total + xrecv[a, n].astype(F32)
         out[...] = total.astype(BF16)
 
-    me = x * 2 + c
-    for p in PARTS:
-        arrived(zhrecv.at[p], zh_r.at[p])
-        fin[me, p] = (zhsend[p].astype(F32) + zhrecv[p].astype(F32)).astype(BF16)
-        for dx in (2, 1, 3, 0):
-            for dc in (1, 0):
-                if dx or dc:
-                    rcopy(fin.at[me, p], fin.at[me, p], ag_s, ag_r.at[p], group(dx, dc)).start()
     for p in PARTS:
         arrived(fin.at[pl.ds(0, 7), p], ag_r.at[p])
 
@@ -393,7 +390,7 @@
     sent(sib_out, sib_s)
     sent(xopp, tro_s)
     sent(xrecv, tr_s)
-    sent(zhsend, zh_s)
+    sent(zhrecv, zh_s)
     sent(fin.at[pl.ds(0, 7)], ag_s)
 
 
@@ -435,14 +432,15 @@
             vm((2, 2, D, ROWS), BF16),
             vm((2, D, ROWS), BF16),
             vm((4, TILES, 16, 128), BF16),
+            vm((D, HID), F32),
             vm((16, sum(WIDE), 16, 128), BF16),
             vm((3, 4, 2, 2, 16, 128), BF16),
             vm((3, 8, 2, 16, 128), BF16),
             vm((3, 2, 16, 128), BF16),
-            vm((3, 2, 16, 128), BF16),
+            vm((3, 2, 2, 16, 128), BF16),
             vm((8, 3, 2, 16, 128), BF16),
             dma((2,)),
-            dma, dma((2,)),
+            dma, dma((2, 2)),
             dma, dma((2, 3)),
             dma, dma((pieces,)),
             dma, dma((pieces,)),
@@ -454,7 +452,6 @@
             dma, dma((3,)),
             dma, dma((3,)),
             dma, dma((3,)),
-            pltpu.SemaphoreType.REGULAR,
         ],
         compiler_params=pltpu.CompilerParams(
             collective_id=0, has_side_effects=True, vmem_limit_bytes=40 << 20

time: 58.6 us -> 56.3 us (0.961)
  Pallas kernels: 57.8 us -> 55.5 us
    pallas_call x1, Pallas kernels: 57 us -> 54.7 us  [per_device(): pl.pallas_call(kernel, out_shape=outs, in_specs=[pl.BlockSpec(memory_spac...]
where the time goes in v7:
time: 56.3 us; the launch traced here: 56.1 us
  Pallas kernels  55.5 us (99%)
  between operations  0.64 us (1%)
    pallas_call x1, Pallas kernels, per_device(): pl.pallas_call(kernel, out_shape=outs, in_specs=[pl.BlockSpec(memory_spac...  54.7 us

profile of v7, /device:TPU:1, one launch (start us, length us, event | category | flops | bytes accessed | tf_op | source)
XLA Modules:
  0.0 56.1 jit_solution(11663182149814508579)
XLA Ops:
  0.6 54.7 %swiglu.1 = (bf16[576,128]{1,0:T(8,128)(2,1)S(1)}, bf16[576,128]{1,0:T(8,128)(2,1)S(1)}, bf16[144,192]{1,0:T(8,128)(2,1)S(1)}, bf16[144,192]{1,0:T(8,128)(2,1)S(1)}, bf16[144,192]{1,0:T(8,128)(2,1)S(1)}) custom-call(bf16[576,128]{1,0:T(8,128)(2,1)} %bitcast.6, bf16[144,192]{1,0:T(8,128)(2,1)} %gate_ref.1, bf16[144,192]{1,0:T(8,128)(2,1)} %up_ref.1, ...), custom_call_target="tpu_custom_call" | custom-call | tf_op jit(solution)/shard_map/swiglu/pallas_call | solution.py:413
  55.3 0.8 %place.1 = (bf16[576,128]{1,0:T(8,128)(2,1)}, bf16[576,128]{1,0:T(8,128)(2,1)}, bf16[144,192]{1,0:T(8,128)(2,1)}, bf16[144,192]{1,0:T(8,128)(2,1)}, bf16[144,192]{1,0:T(8,128)(2,1)}) custom-call(bf16[576,128]{1,0:T(8,128)(2,1)S(1)} %get-tuple-element.15.refs_0_, bf16[576,128]{1,0:T(8,128)(2,1)S(1)} %get-tuple-element.16.refs_1_, ...), custom_call_target="tpu_custom_call" | custom-call | tf_op jit(solution)/shard_map/place/pallas_call | solution.py:461

commit v8 on v7

--- a/solution.py
+++ b/solution.py
@@ -225,7 +225,7 @@
         wait_pair(0, dx)
         sums = tn(wall[:, 0 : 2 * HID], pair(0, dx))
         gate_sum, up_sum = sums[0:HID], sums[HID : 2 * HID]
-        sig = jax.nn.sigmoid(gate_sum)
+        sig = 1.0 / (1.0 + jnp.exp(-gate_sum))
         swished = gate_sum * sig
         swi[:, cols] = swished
         slo[:, cols] = up_sum * sig * (1.0 + gate_sum * (1.0 - sig))

time: 56.3 us -> 56.3 us (level)
  no operation moved by 1% of the time
where the time goes in v8:
time: 56.3 us; the launch traced here: 56.1 us
  Pallas kernels  55.5 us (99%)
  between operations  0.64 us (1%)
    pallas_call x1, Pallas kernels, per_device(): pl.pallas_call(kernel, out_shape=outs, in_specs=[pl.BlockSpec(memory_spac...  54.7 us

profile of v8, /device:TPU:1, one launch (start us, length us, event | category | flops | bytes accessed | tf_op | source)
XLA Modules:
  0.0 56.1 jit_solution(5386833096328637842)
XLA Ops:
  0.6 54.7 %swiglu.1 = (bf16[576,128]{1,0:T(8,128)(2,1)S(1)}, bf16[576,128]{1,0:T(8,128)(2,1)S(1)}, bf16[144,192]{1,0:T(8,128)(2,1)S(1)}, bf16[144,192]{1,0:T(8,128)(2,1)S(1)}, bf16[144,192]{1,0:T(8,128)(2,1)S(1)}) custom-call(bf16[576,128]{1,0:T(8,128)(2,1)} %bitcast.6, bf16[144,192]{1,0:T(8,128)(2,1)} %gate_ref.1, bf16[144,192]{1,0:T(8,128)(2,1)} %up_ref.1, ...), custom_call_target="tpu_custom_call" | custom-call | tf_op jit(solution)/shard_map/swiglu/pallas_call | solution.py:413
  55.3 0.8 %place.1 = (bf16[576,128]{1,0:T(8,128)(2,1)}, bf16[576,128]{1,0:T(8,128)(2,1)}, bf16[144,192]{1,0:T(8,128)(2,1)}, bf16[144,192]{1,0:T(8,128)(2,1)}, bf16[144,192]{1,0:T(8,128)(2,1)}) custom-call(bf16[576,128]{1,0:T(8,128)(2,1)S(1)} %get-tuple-element.15.refs_0_, bf16[576,128]{1,0:T(8,128)(2,1)S(1)} %get-tuple-element.16.refs_1_, ...), custom_call_target="tpu_custom_call" | custom-call | tf_op jit(solution)/shard_map/place/pallas_call | solution.py:461
